TPU v7x, 256 devices: a whole 4x4x8 slice. The times are simulated.
256 devices in a mesh: grp: 16 (over x, y), sp: 16 (over z, core).
Axes of the slice: x: 4, y: 4, z: 8, core: 2. Of those that a mesh axis runs over, the one named last changes fastest.
Arguments:
- query_in: bfloat16 [32768, 4096], P(('grp', 'sp')), may hold values from -200 to 200, as said below
- key_in: bfloat16 [32768, 4096], P(('grp', 'sp')), may hold values from -200 to 200, as said below
- value_in: bfloat16 [32768, 4096], P(('grp', 'sp')), may hold values from -6 to 6
- out_cotangent: bfloat16 [32768, 4096], P(('grp', 'sp')), may hold values from -6 to 6
- query_gain: float32 [4096], replicated, may hold values from 0.8 to 2.5
- key_gain: float32 [4096], replicated, may hold values from 0.8 to 2.5
- frames: int32 [16, 4], P('grp'), may hold values from 1 to 21, 32 in all within a row
- slab_group: int32 [16, 16, 16], P('grp', 'sp'), may hold values from 0 to 15, each once within a row
Outputs:
- attn_out: bfloat16 [32768, 4096], P(('grp', 'sp'))
- grad_q: bfloat16 [32768, 4096], P(('grp', 'sp'))
- grad_k: bfloat16 [32768, 4096], P(('grp', 'sp'))
- grad_v: bfloat16 [32768, 4096], P(('grp', 'sp'))
Inputs may be any that keep to these rules, and one draw needn't show every extreme that they name: Each row lists the latent frames of the 4 videos of one group; a row sums to 32 and its largest entry is exactly 21. `slab_group`: for each device's block, the 8-token slabs go one to each group. `query_in`: real values. `key_in`: real values.
All inputs are finite; a program needn't handle non-finite values.
Results may differ from a plain program's by a relative error of at most 0.04.
The roundings to bfloat16 on the way count: a program that leaves them out, or rounds other values in their place, can miss the bound.
Values may be sent and summed in bfloat16 or wider, within the bound.
No kernel may reach another device: no remote copies, remote signals or barrier semaphores. Data moves between devices by JAX's collectives and lax.ppermute only.
A program may use at most 128 MiB of HBM per device.

v0:
```python
import math

import jax
import jax.numpy as jnp
from jax import lax
from jax.sharding import PartitionSpec as P

HDIM = 128
TOK_FRAME = 64


epsilon = 1e-06
masked_value = -1e30


def normalize(values, gain):
    wide = values.astype(jnp.float32)
    factor = lax.rsqrt(jnp.mean(wide * wide, axis=-1, keepdims=True) + epsilon)
    return ((wide * factor * gain).astype(jnp.bfloat16), factor)


def normalize_back(values, gain, factor, upstream):
    wide = values.astype(jnp.float32)
    scaled = gain * upstream.astype(jnp.float32)
    inner = jnp.mean(wide * scaled, axis=-1, keepdims=True)
    return (factor * scaled - wide * factor * factor * factor * inner).astype(jnp.bfloat16)


def video_index(frames, length):
    positions = jnp.arange(length, dtype=jnp.int32)
    video_ends = jnp.cumsum(frames.reshape(-1)) * TOK_FRAME
    return jnp.sum((positions[:, None] >= video_ends[None, :]).astype(jnp.int32), axis=1)


def tile_scores(query_rows, key_rows, query_video, key_video, scaling):
    scores = (
        jnp.einsum("qhd,khd->hqk", query_rows, key_rows, preferred_element_type=jnp.float32)
        * scaling
    )
    return jnp.where((query_video[:, None] == key_video[None, :])[None], scores, masked_value)


def dense_block(query_rows, cot_rows, query_video, keys_all, values_all, video_of, scaling):
    scores = tile_scores(query_rows, keys_all, query_video, video_of, scaling)
    row_max = jnp.max(scores, axis=-1, keepdims=True)
    log_total = row_max + jnp.log(jnp.sum(jnp.exp(scores - row_max), axis=-1, keepdims=True))
    probs = jnp.exp(scores - log_total)
    weights = probs.astype(jnp.bfloat16)
    attended = jnp.einsum(
        "hqk,khd->qhd", weights, values_all, preferred_element_type=jnp.float32
    ).astype(jnp.bfloat16)
    row_dot = jnp.einsum("qhd,qhd->hq", cot_rows, attended, preferred_element_type=jnp.float32)[
        ..., None
    ]
    dweights = jnp.einsum("qhd,khd->hqk", cot_rows, values_all, preferred_element_type=jnp.float32)
    dscores = (probs * (dweights - row_dot)).astype(jnp.bfloat16)
    d_query = (
        jnp.einsum("hqk,khd->qhd", dscores, keys_all, preferred_element_type=jnp.float32) * scaling
    ).astype(jnp.bfloat16)
    d_key = jnp.einsum("hqk,qhd->khd", dscores, query_rows, preferred_element_type=jnp.float32)
    d_value = jnp.einsum("hqk,qhd->khd", weights, cot_rows, preferred_element_type=jnp.float32)
    return (attended, d_query, d_key, d_value)


def attention(query_all, key_all, value_all, cot_all, video_of):
    length, head_count, head_size = query_all.shape
    block_rows = min(512, length)
    scaling = 1.0 / math.sqrt(head_size)

    def advance(block_index, state):
        outputs, d_queries, key_sum, value_sum = state
        first_row = block_index * block_rows
        query_rows = lax.dynamic_slice_in_dim(query_all, first_row, block_rows, 0)
        cot_rows = lax.dynamic_slice_in_dim(cot_all, first_row, block_rows, 0)
        query_video = lax.dynamic_slice_in_dim(video_of, first_row, block_rows, 0)
        attended, d_query, d_key, d_value = dense_block(
            query_rows, cot_rows, query_video, key_all, value_all, video_of, scaling
        )
        outputs = lax.dynamic_update_slice_in_dim(outputs, attended, first_row, 0)
        d_queries = lax.dynamic_update_slice_in_dim(d_queries, d_query, first_row, 0)
        return (outputs, d_queries, key_sum + d_key, value_sum + d_value)

    start_state = (
        jnp.zeros(query_all.shape, jnp.bfloat16),
        jnp.zeros(query_all.shape, jnp.bfloat16),
        jnp.zeros(query_all.shape, jnp.float32),
        jnp.zeros(query_all.shape, jnp.float32),
    )
    final = lax.fori_loop(0, length // block_rows, advance, start_state)
    return (
        final[0],
        final[1],
        (final[2] * scaling).astype(jnp.bfloat16),
        final[3].astype(jnp.bfloat16),
    )


def local(query_in, key_in, value_in, out_cotangent, query_gain, key_gain, frames, slab_group):
    token_count, features = query_in.shape
    groups = lax.axis_size("grp")
    sp_ways = lax.axis_size("sp")
    slab_rows = token_count // groups
    query_norm, query_factor = normalize(query_in, query_gain)
    key_norm, key_factor = normalize(key_in, key_gain)
    destination = slab_group.reshape(groups)
    slots = jnp.arange(groups, dtype=jnp.int32)
    inverse = jnp.sum(jnp.where(destination[:, None] == slots[None, :], slots[:, None], 0), axis=0)

    def arrange(values):
        return jnp.take(values.reshape(groups, slab_rows, features), inverse, axis=0).reshape(
            token_count, features
        )

    placed = (
        lax.all_to_all(arrange(query_norm), "grp", split_axis=0, concat_axis=0, tiled=True),
        lax.all_to_all(arrange(key_norm), "grp", split_axis=0, concat_axis=0, tiled=True),
        lax.all_to_all(arrange(value_in), "grp", split_axis=0, concat_axis=0, tiled=True),
        lax.all_to_all(arrange(out_cotangent), "grp", split_axis=0, concat_axis=0, tiled=True),
    )
    query_heads, key_heads, value_heads, cot_heads = (
        lax.all_to_all(placed[0], "sp", split_axis=1, concat_axis=0, tiled=True),
        lax.all_to_all(placed[1], "sp", split_axis=1, concat_axis=0, tiled=True),
        lax.all_to_all(placed[2], "sp", split_axis=1, concat_axis=0, tiled=True),
        lax.all_to_all(placed[3], "sp", split_axis=1, concat_axis=0, tiled=True),
    )
    length, head_width = query_heads.shape
    head_count = head_width // HDIM

    def split_heads(values):
        return values.reshape(length, head_count, HDIM)

    video_of = video_index(frames, length)
    attended, d_query, d_key, d_value = attention(
        split_heads(query_heads),
        split_heads(key_heads),
        split_heads(value_heads),
        split_heads(cot_heads),
        video_of,
    )

    def back_shape(values):
        return values.reshape(sp_ways, groups, slab_rows, head_width)

    regrouped = (
        lax.all_to_all(back_shape(attended), "grp", split_axis=1, concat_axis=1, tiled=True),
        lax.all_to_all(back_shape(d_query), "grp", split_axis=1, concat_axis=1, tiled=True),
        lax.all_to_all(back_shape(d_key), "grp", split_axis=1, concat_axis=1, tiled=True),
        lax.all_to_all(back_shape(d_value), "grp", split_axis=1, concat_axis=1, tiled=True),
    )
    returned = (
        lax.all_to_all(regrouped[0], "sp", split_axis=0, concat_axis=3, tiled=True),
        lax.all_to_all(regrouped[1], "sp", split_axis=0, concat_axis=3, tiled=True),
        lax.all_to_all(regrouped[2], "sp", split_axis=0, concat_axis=3, tiled=True),
        lax.all_to_all(regrouped[3], "sp", split_axis=0, concat_axis=3, tiled=True),
    )

    def restore(values):
        return jnp.take(values.reshape(groups, slab_rows, features), destination, axis=0).reshape(
            token_count, features
        )

    attn_out = restore(returned[0])
    grad_q = normalize_back(query_in, query_gain, query_factor, restore(returned[1]))
    grad_k = normalize_back(key_in, key_gain, key_factor, restore(returned[2]))
    grad_v = restore(returned[3])
    return (attn_out, grad_q, grad_k, grad_v)


def solution(mesh):
    return jax.shard_map(
        local,
        mesh=mesh,
        in_specs=(
            P(("grp", "sp"), None),
            P(("grp", "sp"), None),
            P(("grp", "sp"), None),
            P(("grp", "sp"), None),
            P(),
            P(),
            P("grp", None),
            P("grp", "sp", None),
        ),
        out_specs=(
            P(("grp", "sp"), None),
            P(("grp", "sp"), None),
            P(("grp", "sp"), None),
            P(("grp", "sp"), None),
        ),
        check_vma=False,
    )
```

profile of v0, /device:TPU:1, one launch (start us, length us, event | category | flops | bytes accessed | tf_op | source)
XLA Modules:
  0.0 576.9 jit_solution(16659187888924469226)
XLA Ops:
  18.2 23.2 %all_to_all.168 = bf16[16,8,4096]{2,1,0:T(8,128)(2,1)S(1)} all-to-all(bf16[16,8,4096]{2,1,0:T(8,128)(2,1)S(1)} %get-tuple-element.297), channel_id=1, replica_groups=mesh['grp'=16,'sp'=16] {'grp'}, dimensions={0} | all-to-all | bytes 2097152 | tf_op jit(solution)/shard_map/all_to_all | solution.py:116
  41.4 18.4 %all_to_all.169 = bf16[16,8,4096]{2,1,0:T(8,128)(2,1)S(1)} all-to-all(bf16[16,8,4096]{2,1,0:T(8,128)(2,1)S(1)} %get-tuple-element.298), channel_id=1, replica_groups=mesh['grp'=16,'sp'=16] {'grp'}, dimensions={0} | all-to-all | bytes 2097152 | tf_op jit(solution)/shard_map/all_to_all | solution.py:117
  59.8 16.6 %all_to_all.170 = bf16[16,8,4096]{2,1,0:T(8,128)(2,1)} all-to-all(bf16[16,8,4096]{2,1,0:T(8,128)(2,1)S(1)} %get-tuple-element.299), channel_id=1, replica_groups=mesh['grp'=16,'sp'=16] {'grp'}, dimensions={0} | all-to-all | bytes 2097152 | tf_op jit(solution)/shard_map/all_to_all | solution.py:115
  81.8 10.4 %all-to-all-done.6 = bf16[16,8,4096]{2,1,0:T(8,128)(2,1)S(1)} async-done(((bf16[16,8,4096]{2,1,0:T(8,128)(2,1)}), bf16[16,8,4096]{2,1,0:T(8,128)(2,1)S(1)}, u32[]{:S(2)}, u32[]{:S(2)}) %all-to-all-start.6) | async-done | bytes 1048608 | tf_op jit(solution)/shard_map/all_to_all | solution.py:118
  92.3 14.6 %all-to-all-start.3 = ((bf16[128,16,256]{2,0,1:T(8,128)(2,1)}), bf16[128,16,256]{2,0,1:T(8,128)(2,1)S(1)}, u32[]{:S(2)}, u32[]{:S(2)}) async-start(bf16[128,16,256]{2,0,1:T(8,128)(2,1)} %copy.102), calls=%async_computation.3 | async-start | bytes 2097152 | tf_op jit(solution)/shard_map/all_to_all | solution.py:122
  108.5 26.4 %all-to-all-done.3 = bf16[128,16,256]{2,0,1:T(8,128)(2,1)S(1)} async-done(((bf16[128,16,256]{2,0,1:T(8,128)(2,1)}), bf16[128,16,256]{2,0,1:T(8,128)(2,1)S(1)}, u32[]{:S(2)}, u32[]{:S(2)}) %all-to-all-start.3) | async-done | bytes 1048608 | tf_op jit(solution)/shard_map/all_to_all | solution.py:122
  141.2 25.1 %all-to-all-done.5 = bf16[128,16,256]{2,0,1:T(8,128)(2,1)S(1)} async-done(((bf16[128,16,256]{2,0,1:T(8,128)(2,1)}), bf16[128,16,256]{2,0,1:T(8,128)(2,1)S(1)}, u32[]{:S(2)}, u32[]{:S(2)}) %all-to-all-start.5) | async-done | bytes 1048608 | tf_op jit(solution)/shard_map/all_to_all | solution.py:123
  172.2 25.7 %all-to-all-done.1 = bf16[128,16,256]{2,0,1:T(8,128)(2,1)} async-done(((bf16[128,16,256]{2,0,1:T(8,128)(2,1)}), bf16[128,16,256]{2,0,1:T(8,128)(2,1)}, u32[]{:S(2)}, u32[]{:S(2)}) %all-to-all-start.1) | async-done | bytes 1048608 | tf_op jit(solution)/shard_map/all_to_all | solution.py:121
  211.5 17.9 %all-to-all-done.7 = bf16[128,16,256]{2,0,1:T(8,128)(2,1)} async-done(((bf16[128,16,256]{2,0,1:T(8,128)(2,1)}), bf16[128,16,256]{2,0,1:T(8,128)(2,1)}, u32[]{:S(2)}, u32[]{:S(2)}) %all-to-all-start.7) | async-done | bytes 1048608 | tf_op jit(solution)/shard_map/all_to_all | solution.py:124
  234.3 112.8 %while.20 = (s32[]{:T(128)}, bf16[2048,2,128]{2,1,0:T(2,128)(2,1)}, bf16[2048,2,128]{2,1,0:T(2,128)(2,1)}, f32[2048,2,128]{0,2,1:T(8,128)S(1)}, f32[2048,2,128]{...) while((s32[]{:T(128)}, bf16[2048,2,128]{2,1,0:T(2,128)(2,1)}, ...), condition=%wide.region_8.10_spmd.clone, body=%wide.region_5.9_spmd.clone.sunk | while | flops 3269326848 | bytes 153938288 | solution.py:89
  244.6 7.6 %fusion.71 = f32[2048,2,128]{0,2,1:T(8,128)} fusion(f32[2048,2,128]{0,2,1:T(8,128)} %get-tuple-element.393, pred[]{:T(512)S(6)} %compare.3, bf16[512,2,128]{2,1,0:T(2,128)(2,1)} %constant_dynamic-slice_fusion.5, f32[2,512,2048]{2,1,0:T(8,128)} %copy-done.2, f32[2,512]{1,0:T(2,128)S(1)} %log_add_fusion.2, ...), kind=kOutput, calls=%fused_computation.15.clone.1 | convolution fusion | flops 546308096 | bytes 13897729 | tf_op jit(solution)/shard_map/while/body/eval_jaxpr/hqk,qhd->khd/dot_general | solution.py:61
  272.4 8.2 %fusion.71 = f32[2048,2,128]{0,2,1:T(8,128)} fusion(f32[2048,2,128]{0,2,1:T(8,128)} %get-tuple-element.393, pred[]{:T(512)S(6)} %compare.3, bf16[512,2,128]{2,1,0:T(2,128)(2,1)} %constant_dynamic-slice_fusion.5, f32[2,512,2048]{2,1,0:T(8,128)} %copy-done.2, f32[2,512]{1,0:T(2,128)S(1)} %log_add_fusion.2, ...), kind=kOutput, calls=%fused_computation.15.clone.1 | convolution fusion | flops 546308096 | bytes 13897729 | tf_op jit(solution)/shard_map/while/body/eval_jaxpr/hqk,qhd->khd/dot_general | solution.py:61
  300.8 8.2 %fusion.71 = f32[2048,2,128]{0,2,1:T(8,128)} fusion(f32[2048,2,128]{0,2,1:T(8,128)} %get-tuple-element.393, pred[]{:T(512)S(6)} %compare.3, bf16[512,2,128]{2,1,0:T(2,128)(2,1)} %constant_dynamic-slice_fusion.5, f32[2,512,2048]{2,1,0:T(8,128)} %copy-done.2, f32[2,512]{1,0:T(2,128)S(1)} %log_add_fusion.2, ...), kind=kOutput, calls=%fused_computation.15.clone.1 | convolution fusion | flops 546308096 | bytes 13897729 | tf_op jit(solution)/shard_map/while/body/eval_jaxpr/hqk,qhd->khd/dot_general | solution.py:61
  329.1 8.2 %fusion.71 = f32[2048,2,128]{0,2,1:T(8,128)} fusion(f32[2048,2,128]{0,2,1:T(8,128)} %get-tuple-element.393, pred[]{:T(512)S(6)} %compare.3, bf16[512,2,128]{2,1,0:T(2,128)(2,1)} %constant_dynamic-slice_fusion.5, f32[2,512,2048]{2,1,0:T(8,128)} %copy-done.2, f32[2,512]{1,0:T(2,128)S(1)} %log_add_fusion.2, ...), kind=kOutput, calls=%fused_computation.15.clone.1 | convolution fusion | flops 546308096 | bytes 13897729 | tf_op jit(solution)/shard_map/while/body/eval_jaxpr/hqk,qhd->khd/dot_general | solution.py:61
  355.4 15.5 %all-to-all-done.12 = bf16[16,16,8,256]{3,2,0,1:T(8,128)(2,1)S(1)} async-done(((bf16[16,16,8,256]{3,2,0,1:T(8,128)(2,1)}), bf16[16,16,8,256]{3,2,0,1:T(8,128)(2,1)S(1)}, u32[]{:S(2)}, u32[]{:S(2)}) %all-to-all-start.12) | async-done | bytes 1048608 | tf_op jit(solution)/shard_map/all_to_all | solution.py:147
  381.1 11.6 %all-to-all-done.10 = bf16[16,16,8,256]{3,2,0,1:T(8,128)(2,1)S(1)} async-done(((bf16[16,16,8,256]{3,2,0,1:T(8,128)(2,1)}), bf16[16,16,8,256]{3,2,0,1:T(8,128)(2,1)S(1)}, u32[]{:S(2)}, u32[]{:S(2)}) %all-to-all-start.10) | async-done | bytes 1048608 | tf_op jit(solution)/shard_map/all_to_all | solution.py:146
  401.2 10.7 %all-to-all-done.14 = bf16[16,16,8,256]{3,2,0,1:T(8,128)(2,1)S(1)} async-done(((bf16[16,16,8,256]{3,2,0,1:T(8,128)(2,1)}), bf16[16,16,8,256]{3,2,0,1:T(8,128)(2,1)S(1)}, u32[]{:S(2)}, u32[]{:S(2)}) %all-to-all-start.14) | async-done | bytes 1048608 | tf_op jit(solution)/shard_map/all_to_all | solution.py:148
  417.3 13.2 %all-to-all-done.8 = bf16[16,16,8,256]{3,2,0,1:T(8,128)(2,1)} async-done(((bf16[16,16,8,256]{3,2,0,1:T(8,128)(2,1)}), bf16[16,16,8,256]{3,2,0,1:T(8,128)(2,1)}, u32[]{:S(2)}, u32[]{:S(2)}) %all-to-all-start.8) | async-done | bytes 1048608 | tf_op jit(solution)/shard_map/all_to_all | solution.py:145
  430.5 7.4 %all-to-all-start.13 = ((bf16[16,16,8,256]{3,2,1,0:T(8,128)(2,1)}), bf16[16,16,8,256]{3,2,1,0:T(8,128)(2,1)S(1)}, u32[]{:S(2)}, u32[]{:S(2)}) async-start(bf16[16,16,8,256]{3,2,1,0:T(8,128)(2,1)} %copy.122), calls=%async_computation.13 | async-start | bytes 2097152 | tf_op jit(solution)/shard_map/all_to_all | solution.py:153
  439.0 26.9 %all-to-all-done.13 = bf16[16,16,8,256]{3,2,1,0:T(8,128)(2,1)S(1)} async-done(((bf16[16,16,8,256]{3,2,1,0:T(8,128)(2,1)}), bf16[16,16,8,256]{3,2,1,0:T(8,128)(2,1)S(1)}, u32[]{:S(2)}, u32[]{:S(2)}) %all-to-all-start.13) | async-done | bytes 1048608 | tf_op jit(solution)/shard_map/all_to_all | solution.py:153
  470.6 26.8 %all-to-all-done.11 = bf16[16,16,8,256]{3,2,1,0:T(8,128)(2,1)S(1)} async-done(((bf16[16,16,8,256]{3,2,1,0:T(8,128)(2,1)}), bf16[16,16,8,256]{3,2,1,0:T(8,128)(2,1)S(1)}, u32[]{:S(2)}, u32[]{:S(2)}) %all-to-all-start.11) | async-done | bytes 1048608 | tf_op jit(solution)/shard_map/all_to_all | solution.py:152
  503.2 25.6 %all-to-all-done.15 = bf16[16,16,8,256]{3,2,1,0:T(8,128)(2,1)S(1)} async-done(((bf16[16,16,8,256]{3,2,1,0:T(8,128)(2,1)}), bf16[16,16,8,256]{3,2,1,0:T(8,128)(2,1)S(1)}, u32[]{:S(2)}, u32[]{:S(2)}) %all-to-all-start.15) | async-done | bytes 1048608 | tf_op jit(solution)/shard_map/all_to_all | solution.py:154
  542.5 17.9 %all-to-all-done.9 = bf16[16,16,8,256]{3,2,1,0:T(8,128)(2,1)} async-done(((bf16[16,16,8,256]{3,2,1,0:T(8,128)(2,1)}), bf16[16,16,8,256]{3,2,1,0:T(8,128)(2,1)}, u32[]{:S(2)}, u32[]{:S(2)}) %all-to-all-start.9) | async-done | bytes 1048608 | tf_op jit(solution)/shard_map/all_to_all | solution.py:151
  570.9 4.5 fusion.22
  (225 shorter events, 204.6 us)
Async XLA Ops:
  0.6 10.4 %copy-start = (bf16[128,4096]{1,0:T(8,128)(2,1)S(1)}, bf16[128,4096]{1,0:T(8,128)(2,1)}, u32[]{:S(2)}) copy-start(bf16[128,4096]{1,0:T(8,128)(2,1)} %param.14) | copy-start | bytes 3145732
  76.5 15.8 %all-to-all-start.6 = ((bf16[16,8,4096]{2,1,0:T(8,128)(2,1)}), bf16[16,8,4096]{2,1,0:T(8,128)(2,1)S(1)}, u32[]{:S(2)}, u32[]{:S(2)}) async-start(bf16[16,8,4096]{2,1,0:T(8,128)(2,1)} %get-tuple-element.296), calls=%async_computation.6 | async-start | bytes 2097152 | tf_op jit(solution)/shard_map/all_to_all | solution.py:118
  92.3 42.6 %all-to-all-start.3 = ((bf16[128,16,256]{2,0,1:T(8,128)(2,1)}), bf16[128,16,256]{2,0,1:T(8,128)(2,1)S(1)}, u32[]{:S(2)}, u32[]{:S(2)}) async-start(bf16[128,16,256]{2,0,1:T(8,128)(2,1)} %copy.102), calls=%async_computation.3 | async-start | bytes 2097152 | tf_op jit(solution)/shard_map/all_to_all | solution.py:122
  134.8 31.5 %all-to-all-start.5 = ((bf16[128,16,256]{2,0,1:T(8,128)(2,1)}), bf16[128,16,256]{2,0,1:T(8,128)(2,1)S(1)}, u32[]{:S(2)}, u32[]{:S(2)}) async-start(bf16[128,16,256]{2,0,1:T(8,128)(2,1)} %copy.104), calls=%async_computation.5 | async-start | bytes 2097152 | tf_op jit(solution)/shard_map/all_to_all | solution.py:123
  166.3 31.6 %all-to-all-start.1 = ((bf16[128,16,256]{2,0,1:T(8,128)(2,1)}), bf16[128,16,256]{2,0,1:T(8,128)(2,1)}, u32[]{:S(2)}, u32[]{:S(2)}) async-start(bf16[128,16,256]{2,0,1:T(8,128)(2,1)} %copy.100), calls=%async_computation.1 | async-start | bytes 2097152 | tf_op jit(solution)/shard_map/all_to_all | solution.py:121
  170.8 31.3 %copy-start.31 = (s32[1,4]{1,0:T(1,128)S(1)}, s32[1,4]{1,0:T(1,128)}, u32[]{:S(2)}) copy-start(s32[1,4]{1,0:T(1,128)} %param.18) | copy-start | bytes 52
  197.9 31.6 %all-to-all-start.7 = ((bf16[128,16,256]{2,0,1:T(8,128)(2,1)}), bf16[128,16,256]{2,0,1:T(8,128)(2,1)}, u32[]{:S(2)}, u32[]{:S(2)}) async-start(bf16[128,16,256]{2,0,1:T(8,128)(2,1)} %copy.106), calls=%async_computation.7 | async-start | bytes 2097152 | tf_op jit(solution)/shard_map/all_to_all | solution.py:124
  272.4 8.2 %copy-start.10 = (bf16[512,2,128]{2,1,0:T(2,128)(2,1)S(1)}, bf16[512,2,128]{2,1,0:T(2,128)(2,1)}, u32[]{:S(2)}) copy-start(bf16[512,2,128]{2,1,0:T(2,128)(2,1)} %constant_dynamic-slice_fusion.5) | copy-start | bytes 786436 | tf_op jit(solution)/shard_map/while
  272.4 8.2 %copy-start.22 = (bf16[2048,2,128]{2,0,1:T(8,128)(2,1)S(1)}, bf16[2048,2,128]{2,0,1:T(8,128)(2,1)}, u32[]{:S(2)}) copy-start(bf16[2048,2,128]{2,0,1:T(8,128)(2,1)} %get-tuple-element.411) | copy-start | bytes 3145732 | tf_op jit(solution)/shard_map/while
  300.8 8.2 %copy-start.10 = (bf16[512,2,128]{2,1,0:T(2,128)(2,1)S(1)}, bf16[512,2,128]{2,1,0:T(2,128)(2,1)}, u32[]{:S(2)}) copy-start(bf16[512,2,128]{2,1,0:T(2,128)(2,1)} %constant_dynamic-slice_fusion.5) | copy-start | bytes 786436 | tf_op jit(solution)/shard_map/while
  300.8 8.2 %copy-start.22 = (bf16[2048,2,128]{2,0,1:T(8,128)(2,1)S(1)}, bf16[2048,2,128]{2,0,1:T(8,128)(2,1)}, u32[]{:S(2)}) copy-start(bf16[2048,2,128]{2,0,1:T(8,128)(2,1)} %get-tuple-element.411) | copy-start | bytes 3145732 | tf_op jit(solution)/shard_map/while
  329.1 8.2 %copy-start.10 = (bf16[512,2,128]{2,1,0:T(2,128)(2,1)S(1)}, bf16[512,2,128]{2,1,0:T(2,128)(2,1)}, u32[]{:S(2)}) copy-start(bf16[512,2,128]{2,1,0:T(2,128)(2,1)} %constant_dynamic-slice_fusion.5) | copy-start | bytes 786436 | tf_op jit(solution)/shard_map/while
  329.1 8.2 %copy-start.22 = (bf16[2048,2,128]{2,0,1:T(8,128)(2,1)S(1)}, bf16[2048,2,128]{2,0,1:T(8,128)(2,1)}, u32[]{:S(2)}) copy-start(bf16[2048,2,128]{2,0,1:T(8,128)(2,1)} %get-tuple-element.411) | copy-start | bytes 3145732 | tf_op jit(solution)/shard_map/while
  349.9 21.0 %all-to-all-start.12 = ((bf16[16,16,8,256]{3,2,0,1:T(8,128)(2,1)}), bf16[16,16,8,256]{3,2,0,1:T(8,128)(2,1)S(1)}, u32[]{:S(2)}, u32[]{:S(2)}) async-start(bf16[16,16,8,256]{3,2,0,1:T(8,128)(2,1)} %copy.121), calls=%async_computation.12 | async-start | bytes 2097152 | tf_op jit(solution)/shard_map/all_to_all | solution.py:147
  370.9 21.8 %all-to-all-start.10 = ((bf16[16,16,8,256]{3,2,0,1:T(8,128)(2,1)}), bf16[16,16,8,256]{3,2,0,1:T(8,128)(2,1)S(1)}, u32[]{:S(2)}, u32[]{:S(2)}) async-start(bf16[16,16,8,256]{3,2,0,1:T(8,128)(2,1)} %copy.117), calls=%async_computation.10 | async-start | bytes 2097152 | tf_op jit(solution)/shard_map/all_to_all | solution.py:146
  392.7 19.2 %all-to-all-start.14 = ((bf16[16,16,8,256]{3,2,0,1:T(8,128)(2,1)}), bf16[16,16,8,256]{3,2,0,1:T(8,128)(2,1)S(1)}, u32[]{:S(2)}, u32[]{:S(2)}) async-start(bf16[16,16,8,256]{3,2,0,1:T(8,128)(2,1)} %copy.125), calls=%async_computation.14 | async-start | bytes 2097152 | tf_op jit(solution)/shard_map/all_to_all | solution.py:148
  411.9 18.6 %all-to-all-start.8 = ((bf16[16,16,8,256]{3,2,0,1:T(8,128)(2,1)}), bf16[16,16,8,256]{3,2,0,1:T(8,128)(2,1)}, u32[]{:S(2)}, u32[]{:S(2)}) async-start(bf16[16,16,8,256]{3,2,0,1:T(8,128)(2,1)} %copy.113), calls=%async_computation.8 | async-start | bytes 2097152 | tf_op jit(solution)/shard_map/all_to_all | solution.py:145
  430.5 35.4 %all-to-all-start.13 = ((bf16[16,16,8,256]{3,2,1,0:T(8,128)(2,1)}), bf16[16,16,8,256]{3,2,1,0:T(8,128)(2,1)S(1)}, u32[]{:S(2)}, u32[]{:S(2)}) async-start(bf16[16,16,8,256]{3,2,1,0:T(8,128)(2,1)} %copy.122), calls=%async_computation.13 | async-start | bytes 2097152 | tf_op jit(solution)/shard_map/all_to_all | solution.py:153
  437.9 31.5 %copy-start.17 = (bf16[16,16,8,256]{3,2,0,1:T(8,128)(2,1)S(1)}, bf16[16,16,8,256]{3,2,0,1:T(8,128)(2,1)}, u32[]{:S(2)}) copy-start(bf16[16,16,8,256]{3,2,0,1:T(8,128)(2,1)} %copy-done.16) | copy-start | bytes 3145732
  465.9 31.5 %all-to-all-start.11 = ((bf16[16,16,8,256]{3,2,1,0:T(8,128)(2,1)}), bf16[16,16,8,256]{3,2,1,0:T(8,128)(2,1)S(1)}, u32[]{:S(2)}, u32[]{:S(2)}) async-start(bf16[16,16,8,256]{3,2,1,0:T(8,128)(2,1)} %copy.118), calls=%async_computation.11 | async-start | bytes 2097152 | tf_op jit(solution)/shard_map/all_to_all | solution.py:152
  497.4 31.5 %all-to-all-start.15 = ((bf16[16,16,8,256]{3,2,1,0:T(8,128)(2,1)}), bf16[16,16,8,256]{3,2,1,0:T(8,128)(2,1)S(1)}, u32[]{:S(2)}, u32[]{:S(2)}) async-start(bf16[16,16,8,256]{3,2,1,0:T(8,128)(2,1)} %copy.126), calls=%async_computation.15 | async-start | bytes 2097152 | tf_op jit(solution)/shard_map/all_to_all | solution.py:154
  500.9 32.2 %copy-start.32 = (s32[1,1,16]{2,1,0:T(1,128)S(1)}, s32[1,1,16]{2,1,0:T(1,128)}, u32[]{:S(2)}) copy-start(s32[1,1,16]{2,1,0:T(1,128)} %param.19) | copy-start | bytes 196
  528.8 31.6 %all-to-all-start.9 = ((bf16[16,16,8,256]{3,2,1,0:T(8,128)(2,1)}), bf16[16,16,8,256]{3,2,1,0:T(8,128)(2,1)}, u32[]{:S(2)}, u32[]{:S(2)}) async-start(bf16[16,16,8,256]{3,2,1,0:T(8,128)(2,1)} %copy.114), calls=%async_computation.9 | async-start | bytes 2097152 | tf_op jit(solution)/shard_map/all_to_all | solution.py:151
  538.0 30.5 %copy-start.8 = (bf16[16,8,4096]{2,1,0:T(8,128)(2,1)}, bf16[16,8,4096]{2,1,0:T(8,128)(2,1)S(1)}, u32[]{:S(2)}) copy-start(bf16[16,8,4096]{2,1,0:T(8,128)(2,1)S(1)} %gather_fusion.6) | copy-start | bytes 3145732
  (37 other events, 154.2 us)
where the time goes:
time: 579 us; the launch traced here: 577 us
  waiting for transfers between devices  254 us (44%)
  local copies, waits for them, and re-layouts  87.5 us (15%)
  matrix products  79 us (14%)
  starting transfers between devices  64.5 us (11%)
  blocking collectives  58.3 us (10%)
  other arithmetic  32.4 us (6%)
    dot_general x4, matrix products, dense_block(): jnp.einsum('hqk,qhd->khd', weights, cot_rows, preferred_element_type=jnp....  32.3 us
    all_to_all x1, waiting for transfers between devices, local(): lax.all_to_all(regrouped[2], 'sp', split_axis=0, concat_axis=3, tiled=True)  26.9 us
    all_to_all x1, waiting for transfers between devices, local(): lax.all_to_all(regrouped[1], 'sp', split_axis=0, concat_axis=3, tiled=True)  26.8 us
    all_to_all x1, waiting for transfers between devices, local(): lax.all_to_all(placed[1], 'sp', split_axis=1, concat_axis=0, tiled=True)  26.4 us
    all_to_all x1, waiting for transfers between devices, local(): lax.all_to_all(placed[0], 'sp', split_axis=1, concat_axis=0, tiled=True)  25.7 us
    all_to_all x1, waiting for transfers between devices, local(): lax.all_to_all(regrouped[3], 'sp', split_axis=0, concat_axis=3, tiled=True)  25.6 us
    all_to_all x1, waiting for transfers between devices, local(): lax.all_to_all(placed[2], 'sp', split_axis=1, concat_axis=0, tiled=True)  25.1 us
    all_to_all x1, blocking collectives, local(): lax.all_to_all(arrange(key_norm), 'grp', split_axis=0, concat_axis=0, til...  23.2 us
  transfers between devices with their start and end apart: 13, of which 13 were waited for; matrix products, arithmetic and copies ran while one was open for 8% of the time, Pallas kernels for 0%

commit v1 on v0

v1 whole, which is shorter than its diff:
```python
import math

import jax
import jax.numpy as jnp
from jax import lax
from jax.experimental import pallas as pl
from jax.experimental.pallas import tpu as pltpu
from jax.sharding import PartitionSpec as P

HDIM = 128
TOK_FRAME = 64
SLAB = 8
WIDTH = 4096
S_GRP = 2048
FRAMES_GRP = 32
NVID = 4
MOSTF = 21
N_GRP = 16
N_SP = 16
BIG = MOSTF * TOK_FRAME
REST = S_GRP - BIG
BIG_ROWS = 192
REST_ROWS = 176
PER_FRAME = TOK_FRAME // SLAB

EPSILON = 1e-06
MASKED = -1e30
SCALING = 1.0 / math.sqrt(HDIM)
LOG2E = math.log2(math.e)
MIB = 1 << 20

BF16 = jnp.bfloat16
F32 = jnp.float32


def rms_factor(wide):
    return lax.rsqrt(jnp.mean(wide * wide, axis=-1, keepdims=True) + EPSILON)


def pack_kernel(dest, q_ref, k_ref, v_ref, c_ref, qg_ref, kg_ref, first_ref, second_ref):
    def normalize(ref, gain_ref):
        wide = ref[0].astype(F32)
        return (wide * rms_factor(wide) * gain_ref[...]).astype(BF16)

    rows = (normalize(q_ref, qg_ref), normalize(k_ref, kg_ref), v_ref[0], c_ref[0])
    for owner in range(N_SP):
        for half, out_ref in enumerate((first_ref, second_ref)):
            start = (2 * owner + half) * HDIM
            for which in range(4):
                out_ref[0, owner, which] = rows[which][:, start : start + HDIM]


def pack(dest, query_in, key_in, value_in, cot, query_gain, key_gain):
    slab = pl.BlockSpec((1, SLAB, WIDTH), lambda j, d: (j, 0, 0))
    gain = pl.BlockSpec((1, WIDTH), lambda j, d: (0, 0))
    sent = pl.BlockSpec((1, N_SP, 4, SLAB, HDIM), lambda j, d: (d[j], 0, 0, 0, 0))
    shape = jax.ShapeDtypeStruct((N_GRP, N_SP, 4, SLAB, HDIM), BF16)
    return pl.pallas_call(
        pack_kernel,
        grid_spec=pltpu.PrefetchScalarGridSpec(
            num_scalar_prefetch=1,
            grid=(N_GRP,),
            in_specs=[slab, slab, slab, slab, gain, gain],
            out_specs=[sent, sent],
        ),
        out_shape=(shape, shape),
        compiler_params=pltpu.CompilerParams(vmem_limit_bytes=16 * MIB),
        name="pack",
    )(dest, query_in, key_in, value_in, cot, query_gain, key_gain)


def attend(q, c, keys, values, same):
    scores = lax.dot_general(q, keys, (((1,), (1,)), ((), ())), preferred_element_type=F32)
    if same is not None:
        scores = jnp.where(same, scores, MASKED)
    row_max = jnp.max(scores, axis=1, keepdims=True)
    grown = jnp.exp2((scores - row_max) * (SCALING * LOG2E))
    probs = grown * (1.0 / jnp.sum(grown, axis=1, keepdims=True))
    weights = probs.astype(BF16)
    attended = jnp.dot(weights, values, preferred_element_type=F32).astype(BF16)
    row_dot = jnp.sum(c.astype(F32) * attended.astype(F32), axis=1, keepdims=True)
    dweights = lax.dot_general(c, values, (((1,), (1,)), ((), ())), preferred_element_type=F32)
    dscores = (probs * (dweights - row_dot)).astype(BF16)
    d_query = jnp.dot(dscores, keys, preferred_element_type=F32) * SCALING
    over_rows = (((0,), (0,)), ((), ()))
    d_key = lax.dot_general(dscores, q, over_rows, preferred_element_type=F32)
    d_value = lax.dot_general(weights, c, over_rows, preferred_element_type=F32)
    return attended, d_query, d_key, d_value


def attention_kernel(frames, x_ref, out_ref, qs, ks, vs, cs, att, dqs, dks, dvs):
    counts = [frames[v] for v in range(NVID)]
    starts = [jnp.int32(0)]
    for v in range(NVID - 1):
        starts.append(starts[-1] + counts[v])
    before = jnp.int32(0)
    for v in range(NVID):
        before = before + jnp.where(counts[v] == MOSTF, starts[v], 0)

    def slot(frame):
        inside = jnp.logical_and(frame >= before, frame < before + MOSTF)
        outside = jnp.where(frame < before, frame + MOSTF, frame)
        return pl.multiple_of(jnp.where(inside, frame - before, outside) * TOK_FRAME, TOK_FRAME)

    for frame in range(FRAMES_GRP):
        rows = pl.ds(slot(frame), TOK_FRAME)
        part = slice((frame % 2) * PER_FRAME, (frame % 2 + 1) * PER_FRAME)
        for which, held in enumerate((qs, ks, vs, cs)):
            block = x_ref[part, frame // 2, which].astype(F32)
            held[rows, :] = block.reshape(TOK_FRAME, HDIM).astype(BF16)
    dks[...] = jnp.zeros_like(dks)
    dvs[...] = jnp.zeros_like(dvs)

    def section(first, length, block_rows, mask):
        def step(t, carry):
            rows = pl.ds(pl.multiple_of(first + t * block_rows, 16), block_rows)
            whole = pl.ds(first, length)
            attended, d_query, d_key, d_value = attend(
                qs[rows, :], cs[rows, :], ks[whole, :], vs[whole, :], mask(t)
            )
            att[rows, :] = attended
            dqs[rows, :] = d_query.astype(BF16)
            dks[whole, :] += d_key
            dvs[whole, :] += d_value
            return carry

        lax.fori_loop(0, length // block_rows, step, 0)

    def video_of(rest_index):
        position = rest_index + jnp.where(rest_index >= before * TOK_FRAME, BIG, 0)
        found = jnp.zeros_like(position)
        for v in range(1, NVID):
            found = found + (position >= starts[v] * TOK_FRAME).astype(jnp.int32)
        return found

    def rest_mask(t):
        down = lax.broadcasted_iota(jnp.int32, (REST_ROWS, 1), 0) + t * REST_ROWS
        across = lax.broadcasted_iota(jnp.int32, (1, REST), 1)
        return video_of(down) == video_of(across)

    section(0, BIG, BIG_ROWS, lambda t: None)
    section(BIG, REST, REST_ROWS, rest_mask)

    for frame in range(FRAMES_GRP):
        rows = pl.ds(slot(frame), TOK_FRAME)
        part = slice((frame % 2) * PER_FRAME, (frame % 2 + 1) * PER_FRAME)
        results = (
            att[rows, :].astype(F32),
            dqs[rows, :].astype(F32),
            dks[rows, :] * SCALING,
            dvs[rows, :],
        )
        for which in range(4):
            block = results[which].reshape(PER_FRAME, SLAB, HDIM)
            out_ref[part, frame // 2, which] = block.astype(BF16)


def attention(frames, received):
    held = pltpu.VMEM((S_GRP, HDIM), BF16)
    total = pltpu.VMEM((S_GRP, HDIM), F32)
    return pl.pallas_call(
        attention_kernel,
        in_specs=[
            pl.BlockSpec(memory_space=pltpu.SMEM),
            pl.BlockSpec(memory_space=pltpu.VMEM),
        ],
        out_specs=pl.BlockSpec(memory_space=pltpu.VMEM),
        out_shape=jax.ShapeDtypeStruct((N_GRP, N_SP, 4, SLAB, HDIM), BF16),
        scratch_shapes=[held, held, held, held, held, held, total, total],
        compiler_params=pltpu.CompilerParams(vmem_limit_bytes=40 * MIB),
        name="attention",
    )(frames, received)


def finish_kernel(
    dest, first_ref, second_ref, q_ref, k_ref, qg_ref, kg_ref, att_ref, gq_ref, gk_ref, gv_ref
):
    def joined(which):
        pieces = []
        for owner in range(N_SP):
            pieces.append(first_ref[0, owner, which])
            pieces.append(second_ref[0, owner, which])
        return jnp.concatenate(pieces, axis=1)

    def normalize_back(ref, gain_ref, upstream):
        wide = ref[0].astype(F32)
        factor = rms_factor(wide)
        scaled = gain_ref[...] * upstream.astype(F32)
        inner = jnp.mean(wide * scaled, axis=-1, keepdims=True)
        return (factor * scaled - wide * (factor * factor * factor * inner)).astype(BF16)

    att_ref[0] = joined(0)
    gq_ref[0] = normalize_back(q_ref, qg_ref, joined(1))
    gk_ref[0] = normalize_back(k_ref, kg_ref, joined(2))
    gv_ref[0] = joined(3)


def finish(dest, first, second, query_in, key_in, query_gain, key_gain):
    slab = pl.BlockSpec((1, SLAB, WIDTH), lambda j, d: (j, 0, 0))
    gain = pl.BlockSpec((1, WIDTH), lambda j, d: (0, 0))
    sent = pl.BlockSpec((1, N_SP, 4, SLAB, HDIM), lambda j, d: (d[j], 0, 0, 0, 0))
    shape = jax.ShapeDtypeStruct((N_GRP, SLAB, WIDTH), BF16)
    return pl.pallas_call(
        finish_kernel,
        grid_spec=pltpu.PrefetchScalarGridSpec(
            num_scalar_prefetch=1,
            grid=(N_GRP,),
            in_specs=[sent, sent, slab, slab, gain, gain],
            out_specs=[slab, slab, slab, slab],
        ),
        out_shape=(shape, shape, shape, shape),
        compiler_params=pltpu.CompilerParams(vmem_limit_bytes=16 * MIB),
        name="finish",
    )(dest, first, second, query_in, key_in, query_gain, key_gain)


def exchange(values):
    flat = values.reshape(N_GRP * N_SP, 4, SLAB, HDIM)
    moved = lax.all_to_all(flat, ("grp", "sp"), split_axis=0, concat_axis=0, tiled=True)
    return moved.reshape(N_GRP, N_SP, 4, SLAB, HDIM)


def local(query_in, key_in, value_in, out_cotangent, query_gain, key_gain, frames, slab_group):
    tokens, width = query_in.shape
    dest = slab_group.reshape(N_GRP)
    counts = frames.reshape(NVID)

    def slabs(values):
        return values.reshape(N_GRP, SLAB, width)

    gains = (query_gain.reshape(1, width), key_gain.reshape(1, width))
    sent = pack(
        dest, slabs(query_in), slabs(key_in), slabs(value_in), slabs(out_cotangent), *gains
    )
    received = [exchange(part) for part in sent]
    results = [attention(counts, part) for part in received]
    returned = [exchange(part) for part in results]
    outputs = finish(dest, returned[0], returned[1], slabs(query_in), slabs(key_in), *gains)
    return tuple(values.reshape(tokens, width) for values in outputs)


def solution(mesh):
    rows = P(("grp", "sp"), None)
    return jax.shard_map(
        local,
        mesh=mesh,
        in_specs=(rows, rows, rows, rows, P(), P(), P("grp", None), P("grp", "sp", None)),
        out_specs=(rows, rows, rows, rows),
        check_vma=False,
    )
```

time: 579 us -> 269 us (0.46)
  waiting for transfers between devices: 254 us -> 69.3 us
  matrix products: 79 us -> 0 us
  local copies, waits for them, and re-layouts: 87.5 us -> 14.1 us
  blocking collectives: 58.3 us -> 130 us
  starting transfers between devices: 64.5 us -> 10.5 us
  Pallas kernels: 0 us -> 43.4 us
  other arithmetic: 32.4 us -> 0 us
    all_to_all x13 -> x2, waiting for transfers between devices: 254 us -> 69.3 us  [exchange(): lax.all_to_all(flat, ('grp', 'sp'), split_axis=0, concat_axis=0, tiled=True)]
    dot_general x24 -> x0, matrix products: 79 us -> none  [the longest x4 32.3 us: dense_block(): jnp.einsum('hqk,qhd->khd', weights, cot_rows, preferred_element_type=jnp....]
    all_to_all x3 -> x2, blocking collectives: 58.3 us -> 130 us  [exchange(): lax.all_to_all(flat, ('grp', 'sp'), split_axis=0, concat_axis=0, tiled=True)]
    all_to_all x13 -> x2, starting transfers between devices: 64.5 us -> 10.5 us  [exchange(): lax.all_to_all(flat, ('grp', 'sp'), split_axis=0, concat_axis=0, tiled=True)]
    pallas_call x0 -> x4, Pallas kernels: none -> 43.4 us  [the longest x2 33.2 us: attention(): pl.pallas_call(attention_kernel, in_specs=[pl.BlockSpec(memory_space=pltp...]
    reshape x16 -> x0, local copies, waits for them, and re-layouts: 22.8 us -> none  [the longest x8 11.2 us: back_shape(): return values.reshape(sp_ways, groups, slab_rows, head_width)]
    all_to_all x12 -> x0, local copies, waits for them, and re-layouts: 16.3 us -> none  [the longest x1 2.78 us: local(): lax.all_to_all(regrouped[0], 'sp', split_axis=0, concat_axis=3, tiled=True)]
    reduce_sum x9 -> x0, other arithmetic: 16.3 us -> none  [the longest x4 9.96 us: dense_block(): jnp.sum(jnp.exp(scores - row_max), axis=-1, keepdims=True)]
  transfers between devices with their start and end apart: 13 -> 2, of which waited for: 13 -> 2; matrix products, arithmetic and copies ran while one was open for 8% -> 0% of each run, Pallas kernels for 0% -> 12%
where the time goes in v1:
time: 269 us; the launch traced here: 268 us
  blocking collectives  130 us (48%)
  waiting for transfers between devices  69.3 us (26%)
  Pallas kernels  43.4 us (16%)
  local copies, waits for them, and re-layouts  14.1 us (5%)
  starting transfers between devices  10.5 us (4%)
    all_to_all x2, blocking collectives, exchange(): lax.all_to_all(flat, ('grp', 'sp'), split_axis=0, concat_axis=0, tiled=True)  130 us
    all_to_all x2, waiting for transfers between devices, exchange(): lax.all_to_all(flat, ('grp', 'sp'), split_axis=0, concat_axis=0, tiled=True)  69.3 us
    pallas_call x2, Pallas kernels, attention(): pl.pallas_call(attention_kernel, in_specs=[pl.BlockSpec(memory_space=pltp...  33.2 us
    unnamed x38, local copies, waits for them, and re-layouts  14.1 us
    all_to_all x2, starting transfers between devices, exchange(): lax.all_to_all(flat, ('grp', 'sp'), split_axis=0, concat_axis=0, tiled=True)  10.5 us
    pallas_call x1, Pallas kernels, finish(): pl.pallas_call(finish_kernel, grid_spec=pltpu.PrefetchScalarGridSpec(num_...  7.18 us
  transfers between devices with their start and end apart: 2, of which 2 were waited for; matrix products, arithmetic and copies ran while one was open for 0% of the time, Pallas kernels for 12%

profile of v1, /device:TPU:1, one launch (start us, length us, event | category | flops | bytes accessed | tf_op | source)
XLA Modules:
  0.0 267.9 jit_solution(12957551012654291496)
XLA Ops:
  0.6 0.0 copy-start.5
  0.6 1.2 copy-done.5
  1.9 1.2 copy-done.7
  3.1 1.2 copy-done.10
  4.3 1.2 copy-done.11
  5.5 0.7 copy-done.12
  6.3 0.7 copy-done.14
  7.0 0.7 copy-done.17
  7.6 3.0 %pack.1 = (bf16[16,16,4,8,128]{4,3,2,1,0:T(8,128)(2,1)S(1)}, bf16[16,16,4,8,128]{4,3,2,1,0:T(8,128)(2,1)S(1)}) custom-call(s32[16]{0:T(128)S(1)} %bitcast.40, bf16[16,8,4096]{2,1,0:T(8,128)(2,1)S(1)} %bitcast.26, bf16[16,8,4096]{2,1,0:T(8,128)(2,1)S(1)} %bitcast.28, bf16[16,8,4096]{2,1,0:T(8,128)(2,1)S(1)} %bitcast.32, bf16[16,8,4096]{2,1,0:T(8,128)(2,1)S(1)} %bitcast.33, ...), custom_call_target="tpu_custom_call" | custom-call | tf_op jit(solution)/shard_map/pack/pallas_call | solution.py:58
  10.7 70.4 %all_to_all.20 = bf16[256,4,8,128]{3,2,1,0:T(8,128)(2,1)} all-to-all(bf16[256,4,8,128]{3,2,1,0:T(8,128)(2,1)S(1)} %bitcast.31), channel_id=1, replica_groups=mesh['grp'=16,'sp'=16] {'grp','sp'}, dimensions={0} | all-to-all | bytes 4194304 | tf_op jit(solution)/shard_map/all_to_all | solution.py:219
  81.1 5.3 %all-to-all-start = ((bf16[256,4,8,128]{3,2,1,0:T(8,128)(2,1)}), bf16[256,4,8,128]{3,2,1,0:T(8,128)(2,1)S(1)}, u32[]{:S(2)}, u32[]{:S(2)}) async-start(bf16[256,4,8,128]{3,2,1,0:T(8,128)(2,1)} %bitcast.30), calls=%async_computation | async-start | bytes 4194304 | tf_op jit(solution)/shard_map/all_to_all | solution.py:219
  86.5 1.6 copy-done.3
  88.1 16.6 %attention.3 = bf16[16,16,4,8,128]{4,3,2,1,0:T(8,128)(2,1)S(1)} custom-call(s32[4]{0:T(128)S(1)} %bitcast.38, bf16[16,16,4,8,128]{4,3,2,1,0:T(8,128)(2,1)S(1)} %bitcast.24), custom_call_target="tpu_custom_call" | custom-call | tf_op jit(solution)/shard_map/attention/pallas_call | solution.py:161
  104.7 1.3 copy-done.2
  106.0 34.5 %all-to-all-done = bf16[256,4,8,128]{3,2,1,0:T(8,128)(2,1)S(1)} async-done(((bf16[256,4,8,128]{3,2,1,0:T(8,128)(2,1)}), bf16[256,4,8,128]{3,2,1,0:T(8,128)(2,1)S(1)}, u32[]{:S(2)}, u32[]{:S(2)}) %all-to-all-start) | async-done | bytes 2097184 | tf_op jit(solution)/shard_map/all_to_all | solution.py:219
  140.5 1.3 copy-done
  141.8 5.2 %all-to-all-start.3 = ((bf16[256,4,8,128]{3,2,1,0:T(8,128)(2,1)}), bf16[256,4,8,128]{3,2,1,0:T(8,128)(2,1)S(1)}, u32[]{:S(2)}, u32[]{:S(2)}) async-start(bf16[256,4,8,128]{3,2,1,0:T(8,128)(2,1)} %bitcast.23), calls=%async_computation.3 | async-start | bytes 4194304 | tf_op jit(solution)/shard_map/all_to_all | solution.py:219
  147.0 1.6 copy-done.1
  148.6 16.6 %attention.2 = bf16[16,16,4,8,128]{4,3,2,1,0:T(8,128)(2,1)S(1)} custom-call(s32[4]{0:T(128)S(1)} %bitcast.39, bf16[16,16,4,8,128]{4,3,2,1,0:T(8,128)(2,1)S(1)} %bitcast.22), custom_call_target="tpu_custom_call" | custom-call | tf_op jit(solution)/shard_map/attention/pallas_call | solution.py:161
  165.2 1.3 copy-done.4
  166.5 34.7 %all-to-all-done.3 = bf16[256,4,8,128]{3,2,1,0:T(8,128)(2,1)S(1)} async-done(((bf16[256,4,8,128]{3,2,1,0:T(8,128)(2,1)}), bf16[256,4,8,128]{3,2,1,0:T(8,128)(2,1)S(1)}, u32[]{:S(2)}, u32[]{:S(2)}) %all-to-all-start.3) | async-done | bytes 2097184 | tf_op jit(solution)/shard_map/all_to_all | solution.py:219
  201.3 0.0 copy-start.18
  201.3 59.4 %all_to_all.21 = bf16[256,4,8,128]{3,2,1,0:T(8,128)(2,1)S(1)} all-to-all(bf16[256,4,8,128]{3,2,1,0:T(8,128)(2,1)} %bitcast.25), channel_id=1, replica_groups=mesh['grp'=16,'sp'=16] {'grp','sp'}, dimensions={0} | all-to-all | bytes 4194304 | tf_op jit(solution)/shard_map/all_to_all | solution.py:219
  260.7 7.2 %finish.1 = (bf16[16,8,4096]{2,1,0:T(8,128)(2,1)}, bf16[16,8,4096]{2,1,0:T(8,128)(2,1)}, bf16[16,8,4096]{2,1,0:T(8,128)(2,1)}, bf16[16,8,4096]{2,1,0:T(8,128)(2,1)}) custom-call(s32[16]{0:T(128)S(1)} %bitcast.41, bf16[16,16,4,8,128]{4,3,2,1,0:T(8,128)(2,1)S(1)} %bitcast.21, bf16[16,16,4,8,128]{4,3,2,1,0:T(8,128)(2,1)S(1)} %bitcast.20, ...), custom_call_target="tpu_custom_call" | custom-call | tf_op jit(solution)/shard_map/finish/pallas_call | solution.py:203
  (24 shorter events, 0.0 us)
Async XLA Ops:
  0.6 1.2 copy-start.5
  1.9 1.2 copy-start.7
  3.1 1.2 copy-start.10
  4.3 1.2 copy-start.11
  5.5 0.7 copy-start.12
  6.3 0.7 copy-start.14
  7.0 0.7 copy-start.17
  10.7 70.5 %copy-start.9 = (bf16[16,16,4,8,128]{4,3,2,1,0:T(8,128)(2,1)}, bf16[16,16,4,8,128]{4,3,2,1,0:T(8,128)(2,1)S(1)}, u32[]{:S(2)}) copy-start(bf16[16,16,4,8,128]{4,3,2,1,0:T(8,128)(2,1)S(1)} %get-tuple-element.10) | copy-start | bytes 6291460
  81.1 5.3 %copy-start.16 = (s32[1,4]{1,0:T(1,128)S(1)}, s32[1,4]{1,0:T(1,128)}, u32[]{:S(2)}) copy-start(s32[1,4]{1,0:T(1,128)} %param.14) | copy-start | bytes 52
  81.1 59.4 %all-to-all-start = ((bf16[256,4,8,128]{3,2,1,0:T(8,128)(2,1)}), bf16[256,4,8,128]{3,2,1,0:T(8,128)(2,1)S(1)}, u32[]{:S(2)}, u32[]{:S(2)}) async-start(bf16[256,4,8,128]{3,2,1,0:T(8,128)(2,1)} %bitcast.30), calls=%async_computation | async-start | bytes 4194304 | tf_op jit(solution)/shard_map/all_to_all | solution.py:219
  86.5 1.6 copy-start.3
  104.7 1.3 copy-start.2
  140.5 1.3 copy-start
  141.8 59.4 %all-to-all-start.3 = ((bf16[256,4,8,128]{3,2,1,0:T(8,128)(2,1)}), bf16[256,4,8,128]{3,2,1,0:T(8,128)(2,1)S(1)}, u32[]{:S(2)}, u32[]{:S(2)}) async-start(bf16[256,4,8,128]{3,2,1,0:T(8,128)(2,1)} %bitcast.23), calls=%async_computation.3 | async-start | bytes 4194304 | tf_op jit(solution)/shard_map/all_to_all | solution.py:219
  147.0 1.6 copy-start.1
  165.2 1.3 copy-start.4
  201.3 59.4 %copy-start.6 = (bf16[128,4096]{1,0:T(8,128)(2,1)S(1)}, bf16[128,4096]{1,0:T(8,128)(2,1)}, u32[]{:S(2)}) copy-start(bf16[128,4096]{1,0:T(8,128)(2,1)} %param.8) | copy-start | bytes 3145732
  201.3 59.4 %copy-start.8 = (bf16[128,4096]{1,0:T(8,128)(2,1)S(1)}, bf16[128,4096]{1,0:T(8,128)(2,1)}, u32[]{:S(2)}) copy-start(bf16[128,4096]{1,0:T(8,128)(2,1)} %param.9) | copy-start | bytes 3145732
  201.3 59.4 %copy-start.13 = (f32[4096]{0:T(1024)S(1)}, f32[4096]{0:T(1024)}, u32[]{:S(2)}) copy-start(f32[4096]{0:T(1024)} %param.12) | copy-start | bytes 49156
  201.3 59.5 %copy-start.15 = (f32[4096]{0:T(1024)S(1)}, f32[4096]{0:T(1024)}, u32[]{:S(2)}) copy-start(f32[4096]{0:T(1024)} %param.13) | copy-start | bytes 49156
  201.3 59.5 %copy-start.18 = (s32[1,1,16]{2,1,0:T(1,128)S(1)}, s32[1,1,16]{2,1,0:T(1,128)}, u32[]{:S(2)}) copy-start(s32[1,1,16]{2,1,0:T(1,128)} %param.15) | copy-start | bytes 196

commit v2 on v1

v2 whole, which is shorter than its diff:
```python
import math

import jax
import jax.numpy as jnp
from jax import lax
from jax.experimental import pallas as pl
from jax.experimental.pallas import tpu as pltpu
from jax.sharding import PartitionSpec as P

HDIM = 128
TOK_FRAME = 64
SLAB = 8
WIDTH = 4096
S_GRP = 2048
FRAMES_GRP = 32
NVID = 4
MOSTF = 21
N_GRP = 16
N_SP = 16
BIG = MOSTF * TOK_FRAME
REST = S_GRP - BIG
PER_FRAME = TOK_FRAME // SLAB
PAIR = 2 * HDIM
PART = 4

EPSILON = 1e-06
MASKED = -1e30
SCALING = 1.0 / math.sqrt(HDIM)
LOG2E = math.log2(math.e)
MIB = 1 << 20
ATT_VMEM = 40 * MIB

BF16 = jnp.bfloat16
F32 = jnp.float32


def rms_factor(wide):
    return lax.rsqrt(jnp.mean(wide * wide, axis=-1, keepdims=True) + EPSILON)


def pack_kernel(dest, q_ref, k_ref, v_ref, c_ref, qg_ref, kg_ref, out_ref, held, arrived):
    def fetch(which, part):
        source = (q_ref, k_ref, v_ref, c_ref)[which]
        rows = pl.ds(part * PART, PART)
        return pltpu.make_async_copy(
            source.at[rows], held.at[which, rows], arrived.at[which, part]
        )

    for part in range(N_GRP // PART):
        for which in range(4):
            fetch(which, part).start()

    def normalize(values, gain_ref):
        wide = values.astype(F32)
        return (wide * rms_factor(wide) * gain_ref[...]).astype(BF16)

    for part in range(N_GRP // PART):
        for which in range(4):
            fetch(which, part).wait()
        for slab in range(part * PART, (part + 1) * PART):
            rows = (
                normalize(held[0, slab], qg_ref),
                normalize(held[1, slab], kg_ref),
                held[2, slab],
                held[3, slab],
            )
            for owner in range(N_SP):
                for which in range(4):
                    piece = rows[which][:, owner * PAIR : (owner + 1) * PAIR]
                    out_ref[dest[slab], owner, which] = piece


def pack(dest, query_in, key_in, value_in, cot, query_gain, key_gain):
    smem = pl.BlockSpec(memory_space=pltpu.SMEM)
    vmem = pl.BlockSpec(memory_space=pltpu.VMEM)
    hbm = pl.BlockSpec(memory_space=pl.ANY)
    return pl.pallas_call(
        pack_kernel,
        in_specs=[smem, hbm, hbm, hbm, hbm, vmem, vmem],
        out_specs=vmem,
        out_shape=jax.ShapeDtypeStruct((N_GRP, N_SP, 4, SLAB, PAIR), BF16),
        scratch_shapes=[
            pltpu.VMEM((4, N_GRP, SLAB, WIDTH), BF16),
            pltpu.SemaphoreType.DMA((4, N_GRP // PART)),
        ],
        compiler_params=pltpu.CompilerParams(vmem_limit_bytes=32 * MIB),
        name="pack",
    )(dest, query_in, key_in, value_in, cot, query_gain, key_gain)


def attend(q, keys, values, c, same):
    rows = (((1,), (1,)), ((), ()))
    over_rows = (((0,), (0,)), ((), ()))
    scores = lax.dot_general(q, keys, rows, preferred_element_type=F32)
    if same is not None:
        scores = jnp.where(same, scores, MASKED)
    row_max = jnp.max(scores, axis=1, keepdims=True)
    grown = jnp.exp2((scores - row_max) * (SCALING * LOG2E))
    probs = grown * (1.0 / jnp.sum(grown, axis=1, keepdims=True))
    weights = probs.astype(BF16)
    attended = jnp.dot(weights, values, preferred_element_type=F32).astype(BF16)
    row_dot = jnp.sum(c.astype(F32) * attended.astype(F32), axis=1, keepdims=True)
    dweights = lax.dot_general(c, values, rows, preferred_element_type=F32)
    dscores = (probs * (dweights - row_dot)).astype(BF16)
    d_query = jnp.dot(dscores, keys, preferred_element_type=F32) * SCALING
    d_key = lax.dot_general(dscores, q, over_rows, preferred_element_type=F32) * SCALING
    d_value = lax.dot_general(weights, c, over_rows, preferred_element_type=F32)
    return attended, d_query, d_key, d_value


def attention_kernel(frames, x_ref, out_ref, *held):
    counts = [frames[v] for v in range(NVID)]
    starts = [jnp.int32(0)]
    for v in range(NVID - 1):
        starts.append(starts[-1] + counts[v])
    before = jnp.int32(0)
    for v in range(NVID):
        before = before + jnp.where(counts[v] == MOSTF, starts[v], 0)

    def frame_rows(frame):
        inside = jnp.logical_and(frame >= before, frame < before + MOSTF)
        outside = jnp.where(frame < before, frame + MOSTF, frame)
        slot = jnp.where(inside, frame - before, outside) * TOK_FRAME
        return pl.ds(pl.multiple_of(slot, TOK_FRAME), TOK_FRAME)

    def video_of(rest_index):
        position = rest_index + jnp.where(rest_index >= before * TOK_FRAME, BIG, 0)
        found = jnp.zeros_like(position)
        for v in range(1, NVID):
            found = found + (position >= starts[v] * TOK_FRAME).astype(jnp.int32)
        return found

    down = lax.broadcasted_iota(jnp.int32, (REST, 1), 0)
    across = lax.broadcasted_iota(jnp.int32, (1, REST), 1)
    same = video_of(down) == video_of(across)
    slots = [frame_rows(frame) for frame in range(FRAMES_GRP)]

    def slab_rows(frame):
        return slice((frame % 2) * PER_FRAME, (frame % 2 + 1) * PER_FRAME)

    for head in range(2):
        lanes = slice(head * HDIM, (head + 1) * HDIM)
        ins, outs = held[8 * head : 8 * head + 4], held[8 * head + 4 : 8 * head + 8]
        for frame in range(FRAMES_GRP):
            for which in range(4):
                block = x_ref[slab_rows(frame), frame // 2, which, :, lanes].astype(F32)
                ins[which][slots[frame], :] = block.reshape(TOK_FRAME, HDIM).astype(BF16)
        for section, mask in ((slice(0, BIG), None), (slice(BIG, S_GRP), same)):
            results = attend(*(ref[section, :] for ref in ins), mask)
            for which in range(4):
                outs[which][section, :] = results[which].astype(outs[which].dtype)
        for frame in range(FRAMES_GRP):
            for which in range(4):
                block = outs[which][slots[frame], :].astype(F32).reshape(PER_FRAME, SLAB, HDIM)
                out_ref[slab_rows(frame), frame // 2, which, :, lanes] = block.astype(BF16)


def attention(frames, received):
    held = [pltpu.VMEM((S_GRP, HDIM), BF16)] * 16
    return pl.pallas_call(
        attention_kernel,
        in_specs=[
            pl.BlockSpec(memory_space=pltpu.SMEM),
            pl.BlockSpec(memory_space=pltpu.VMEM),
        ],
        out_specs=pl.BlockSpec(memory_space=pltpu.VMEM),
        out_shape=jax.ShapeDtypeStruct((N_GRP, N_SP, 4, SLAB, PAIR), BF16),
        scratch_shapes=held,
        compiler_params=pltpu.CompilerParams(vmem_limit_bytes=ATT_VMEM),
        name="attention",
    )(frames, received)


def finish_kernel(
    dest, x_ref, q_ref, k_ref, qg_ref, kg_ref, att_ref, gq_ref, gk_ref, gv_ref, held, gone
):
    def store(which, part):
        target = (att_ref, gq_ref, gk_ref, gv_ref)[which]
        rows = pl.ds(part * PART, PART)
        return pltpu.make_async_copy(held.at[which, rows], target.at[rows], gone.at[which, part])

    def normalize_back(values, gain_ref, upstream):
        wide = values.astype(F32)
        factor = rms_factor(wide)
        scaled = gain_ref[...] * upstream.astype(F32)
        inner = jnp.mean(wide * scaled, axis=-1, keepdims=True)
        return (factor * scaled - wide * (factor * factor * factor * inner)).astype(BF16)

    for part in range(N_GRP // PART):
        for which in (0, 3):
            for slab in range(part * PART, (part + 1) * PART):
                for owner in range(N_SP):
                    columns = slice(owner * PAIR, (owner + 1) * PAIR)
                    held[which, slab, :, columns] = x_ref[dest[slab], owner, which]
            store(which, part).start()
    for part in range(N_GRP // PART):
        for which, source, gain_ref in ((1, q_ref, qg_ref), (2, k_ref, kg_ref)):
            for slab in range(part * PART, (part + 1) * PART):
                pieces = [x_ref[dest[slab], owner, which] for owner in range(N_SP)]
                upstream = jnp.concatenate(pieces, axis=1)
                held[which, slab] = normalize_back(source[slab], gain_ref, upstream)
            store(which, part).start()
    for part in range(N_GRP // PART):
        for which in range(4):
            store(which, part).wait()


def finish(dest, returned, query_in, key_in, query_gain, key_gain):
    smem = pl.BlockSpec(memory_space=pltpu.SMEM)
    vmem = pl.BlockSpec(memory_space=pltpu.VMEM)
    hbm = pl.BlockSpec(memory_space=pl.ANY)
    return pl.pallas_call(
        finish_kernel,
        in_specs=[smem, vmem, vmem, vmem, vmem, vmem],
        out_specs=[hbm, hbm, hbm, hbm],
        out_shape=[jax.ShapeDtypeStruct((N_GRP, SLAB, WIDTH), BF16)] * 4,
        scratch_shapes=[
            pltpu.VMEM((4, N_GRP, SLAB, WIDTH), BF16),
            pltpu.SemaphoreType.DMA((4, N_GRP // PART)),
        ],
        compiler_params=pltpu.CompilerParams(vmem_limit_bytes=32 * MIB),
        name="finish",
    )(dest, returned, query_in, key_in, query_gain, key_gain)


def exchange(values):
    flat = values.reshape(N_GRP * N_SP, 4, SLAB, PAIR)
    moved = lax.all_to_all(flat, ("grp", "sp"), split_axis=0, concat_axis=0, tiled=True)
    return moved.reshape(values.shape)


def local(query_in, key_in, value_in, out_cotangent, query_gain, key_gain, frames, slab_group):
    tokens, width = query_in.shape
    dest = slab_group.reshape(N_GRP)

    def slabs(values):
        return values.reshape(N_GRP, SLAB, width)

    gains = (query_gain.reshape(1, width), key_gain.reshape(1, width))
    sent = pack(
        dest, slabs(query_in), slabs(key_in), slabs(value_in), slabs(out_cotangent), *gains
    )
    results = attention(frames.reshape(NVID), exchange(sent))
    outputs = finish(dest, exchange(results), slabs(query_in), slabs(key_in), *gains)
    return tuple(values.reshape(tokens, width) for values in outputs)


def solution(mesh):
    rows = P(("grp", "sp"), None)
    return jax.shard_map(
        local,
        mesh=mesh,
        in_specs=(rows, rows, rows, rows, P(), P(), P("grp", None), P("grp", "sp", None)),
        out_specs=(rows, rows, rows, rows),
        check_vma=False,
    )
```

time: 269 us -> 255 us (0.948)
  blocking collectives: 130 us -> 219 us
  waiting for transfers between devices: 69.3 us -> 0 us
  Pallas kernels: 43.4 us -> 27.8 us
  starting transfers between devices: 10.5 us -> 0 us
  local copies, waits for them, and re-layouts: 14.1 us -> 7.02 us
    all_to_all x2, blocking collectives: 130 us -> 219 us  [exchange(): lax.all_to_all(flat, ('grp', 'sp'), split_axis=0, concat_axis=0, tiled=True)]
    all_to_all x2 -> x0, waiting for transfers between devices: 69.3 us -> none  [exchange(): lax.all_to_all(flat, ('grp', 'sp'), split_axis=0, concat_axis=0, tiled=True)]
    pallas_call x2 -> x1, Pallas kernels: 33.2 us -> 21.9 us  [attention(): pl.pallas_call(attention_kernel, in_specs=[pl.BlockSpec(memory_space=pltp...]
    all_to_all x2 -> x0, starting transfers between devices: 10.5 us -> none  [exchange(): lax.all_to_all(flat, ('grp', 'sp'), split_axis=0, concat_axis=0, tiled=True)]
    unnamed x38 -> x26, local copies, waits for them, and re-layouts: 14.1 us -> 7.02 us
    pallas_call x2, Pallas kernels: 10.2 us -> 5.99 us  [the longest x1 3.93 us: finish(): pl.pallas_call(finish_kernel, in_specs=[smem, vmem, vmem, vmem, vmem, vme...]
  transfers between devices with their start and end apart: 2 -> 0, of which waited for: 2 -> 0; matrix products, arithmetic and copies ran while one was open for 0% -> 0% of each run, Pallas kernels for 12% -> 0%
where the time goes in v2:
time: 255 us
  blocking collectives  219 us (86%)
  Pallas kernels  27.8 us (11%)
  local copies, waits for them, and re-layouts  7.02 us (3%)
    all_to_all x2, blocking collectives, exchange(): lax.all_to_all(flat, ('grp', 'sp'), split_axis=0, concat_axis=0, tiled=True)  219 us
    pallas_call x1, Pallas kernels, attention(): pl.pallas_call(attention_kernel, in_specs=[pl.BlockSpec(memory_space=pltp...  21.9 us
    unnamed x26, local copies, waits for them, and re-layouts  7.02 us

profile of v2, /device:TPU:1, one launch (start us, length us, event | category | flops | bytes accessed | tf_op | source)
XLA Modules:
  0.0 255.1 jit_solution(5474957961343583024)
XLA Ops:
  0.6 0.0 copy-start
  0.6 1.2 copy-done
  1.9 1.2 copy-done.2
  3.1 1.2 copy-done.4
  4.3 1.2 copy-done.5
  5.5 0.7 copy-done.6
  6.3 0.7 copy-done.8
  7.0 0.7 copy-done.10
  7.6 2.1 pack.1
  9.7 0.0 copy-start.12
  9.7 115.2 %all_to_all.10 = bf16[256,4,8,256]{3,2,1,0:T(8,128)(2,1)S(1)} all-to-all(bf16[256,4,8,256]{3,2,1,0:T(8,128)(2,1)S(1)} %bitcast.19), channel_id=1, replica_groups=mesh['grp'=16,'sp'=16] {'grp','sp'}, dimensions={0} | all-to-all | bytes 8388608 | tf_op jit(solution)/shard_map/all_to_all | solution.py:228
  124.9 0.0 copy-done.12
  124.9 21.9 %attention.1 = bf16[16,16,4,8,256]{4,3,2,1,0:T(8,128)(2,1)S(1)} custom-call(s32[4]{0:T(128)S(1)} %bitcast.32, bf16[16,16,4,8,256]{4,3,2,1,0:T(8,128)(2,1)S(1)} %bitcast.17), custom_call_target="tpu_custom_call" | custom-call | tf_op jit(solution)/shard_map/attention/pallas_call | solution.py:160
  146.8 0.0 copy-start.1
  146.8 0.0 copy-start.3
  146.8 0.0 copy-start.7
  146.8 0.0 copy-start.9
  146.8 0.0 copy-start.11
  146.8 104.1 %all_to_all.11 = bf16[256,4,8,256]{3,2,1,0:T(8,128)(2,1)S(1)} all-to-all(bf16[256,4,8,256]{3,2,1,0:T(8,128)(2,1)S(1)} %bitcast.18), channel_id=1, replica_groups=mesh['grp'=16,'sp'=16] {'grp','sp'}, dimensions={0} | all-to-all | bytes 8388608 | tf_op jit(solution)/shard_map/all_to_all | solution.py:228
  250.9 0.0 copy-done.1
  250.9 0.0 copy-done.3
  250.9 0.0 copy-done.7
  250.9 0.0 copy-done.9
  250.9 3.9 %finish.1 = (bf16[16,8,4096]{2,1,0:T(8,128)(2,1)}, bf16[16,8,4096]{2,1,0:T(8,128)(2,1)}, bf16[16,8,4096]{2,1,0:T(8,128)(2,1)}, bf16[16,8,4096]{2,1,0:T(8,128)(2,1)}) custom-call(s32[16]{0:T(128)S(1)} %bitcast.31, bf16[16,16,4,8,256]{4,3,2,1,0:T(8,128)(2,1)S(1)} %bitcast.16, bf16[16,8,4096]{2,1,0:T(8,128)(2,1)S(1)} %bitcast.21, ...), custom_call_target="tpu_custom_call" | custom-call | tf_op jit(solution)/shard_map/finish/pallas_call | solution.py:212
  (7 shorter events, 0.0 us)
Async XLA Ops:
  0.6 1.2 copy-start
  1.9 1.2 copy-start.2
  3.1 1.2 copy-start.4
  4.3 1.2 copy-start.5
  5.5 0.7 copy-start.6
  6.3 0.7 copy-start.8
  7.0 0.7 copy-start.10
  9.7 115.2 %copy-start.12 = (s32[1,4]{1,0:T(1,128)S(1)}, s32[1,4]{1,0:T(1,128)}, u32[]{:S(2)}) copy-start(s32[1,4]{1,0:T(1,128)} %param.14) | copy-start | bytes 52
  146.8 104.2 %copy-start.1 = (bf16[128,4096]{1,0:T(8,128)(2,1)S(1)}, bf16[128,4096]{1,0:T(8,128)(2,1)}, u32[]{:S(2)}) copy-start(bf16[128,4096]{1,0:T(8,128)(2,1)} %param.8) | copy-start | bytes 3145732
  146.8 104.1 %copy-start.3 = (bf16[128,4096]{1,0:T(8,128)(2,1)S(1)}, bf16[128,4096]{1,0:T(8,128)(2,1)}, u32[]{:S(2)}) copy-start(bf16[128,4096]{1,0:T(8,128)(2,1)} %param.9) | copy-start | bytes 3145732
  146.8 104.1 %copy-start.7 = (f32[4096]{0:T(1024)S(1)}, f32[4096]{0:T(1024)}, u32[]{:S(2)}) copy-start(f32[4096]{0:T(1024)} %param.12) | copy-start | bytes 49156
  146.8 104.1 %copy-start.9 = (f32[4096]{0:T(1024)S(1)}, f32[4096]{0:T(1024)}, u32[]{:S(2)}) copy-start(f32[4096]{0:T(1024)} %param.13) | copy-start | bytes 49156
  146.8 104.1 %copy-start.11 = (s32[1,1,16]{2,1,0:T(1,128)S(1)}, s32[1,1,16]{2,1,0:T(1,128)}, u32[]{:S(2)}) copy-start(s32[1,1,16]{2,1,0:T(1,128)} %param.15) | copy-start | bytes 196

commit v3 on v2

--- a/solution.py
+++ b/solution.py
@@ -38,7 +38,13 @@
     return lax.rsqrt(jnp.mean(wide * wide, axis=-1, keepdims=True) + EPSILON)
 
 
-def pack_kernel(dest, q_ref, k_ref, v_ref, c_ref, qg_ref, kg_ref, out_ref, held, arrived):
+def pack_kernel(
+    dest, q_ref, k_ref, v_ref, c_ref, qg_hbm, kg_hbm, out_ref, held, qg_ref, kg_ref, arrived, ready
+):
+    gains = (
+        pltpu.make_async_copy(qg_hbm, qg_ref, ready.at[0]),
+        pltpu.make_async_copy(kg_hbm, kg_ref, ready.at[1]),
+    )
     def fetch(which, part):
         source = (q_ref, k_ref, v_ref, c_ref)[which]
         rows = pl.ds(part * PART, PART)
@@ -46,9 +52,13 @@
             source.at[rows], held.at[which, rows], arrived.at[which, part]
         )
 
+    for copy in gains:
+        copy.start()
     for part in range(N_GRP // PART):
         for which in range(4):
             fetch(which, part).start()
+    for copy in gains:
+        copy.wait()
 
     def normalize(values, gain_ref):
         wide = values.astype(F32)
@@ -73,19 +83,26 @@
 def pack(dest, query_in, key_in, value_in, cot, query_gain, key_gain):
     smem = pl.BlockSpec(memory_space=pltpu.SMEM)
     vmem = pl.BlockSpec(memory_space=pltpu.VMEM)
-    hbm = pl.BlockSpec(memory_space=pl.ANY)
+    hbm = pl.BlockSpec(memory_space=pltpu.HBM)
+    operands = [
+        pltpu.with_memory_space_constraint(values, pltpu.HBM)
+        for values in (dest, query_in, key_in, value_in, cot, query_gain, key_gain)
+    ]
     return pl.pallas_call(
         pack_kernel,
-        in_specs=[smem, hbm, hbm, hbm, hbm, vmem, vmem],
+        in_specs=[smem, hbm, hbm, hbm, hbm, hbm, hbm],
         out_specs=vmem,
         out_shape=jax.ShapeDtypeStruct((N_GRP, N_SP, 4, SLAB, PAIR), BF16),
         scratch_shapes=[
             pltpu.VMEM((4, N_GRP, SLAB, WIDTH), BF16),
+            pltpu.VMEM((1, WIDTH), F32),
+            pltpu.VMEM((1, WIDTH), F32),
             pltpu.SemaphoreType.DMA((4, N_GRP // PART)),
+            pltpu.SemaphoreType.DMA((2,)),
         ],
         compiler_params=pltpu.CompilerParams(vmem_limit_bytes=32 * MIB),
         name="pack",
-    )(dest, query_in, key_in, value_in, cot, query_gain, key_gain)
+    )(*operands)
 
 
 def attend(q, keys, values, c, same):

time: 255 us -> 250 us (0.980)
  local copies, waits for them, and re-layouts: 7.02 us -> 0.04 us
    unnamed x26 -> x12, local copies, waits for them, and re-layouts: 7.02 us -> 0.04 us
where the time goes in v3:
time: 250 us
  blocking collectives  219 us (88%)
  Pallas kernels  29.5 us (12%)
    all_to_all x2, blocking collectives, exchange(): lax.all_to_all(flat, ('grp', 'sp'), split_axis=0, concat_axis=0, tiled=True)  219 us
    pallas_call x1, Pallas kernels, attention(): pl.pallas_call(attention_kernel, in_specs=[pl.BlockSpec(memory_space=pltp...  21.9 us

profile of v3, /device:TPU:1, one launch (start us, length us, event | category | flops | bytes accessed | tf_op | source)
XLA Modules:
  0.0 249.7 jit_solution(12733718125144924872)
XLA Ops:
  0.6 3.7 %pack.1 = bf16[16,16,4,8,256]{4,3,2,1,0:T(8,128)(2,1)S(1)} custom-call(s32[16]{0:T(128)} %bitcast.28, bf16[16,8,4096]{2,1,0:T(8,128)(2,1)} %bitcast.20, bf16[16,8,4096]{2,1,0:T(8,128)(2,1)} %bitcast.22, bf16[16,8,4096]{2,1,0:T(8,128)(2,1)} %bitcast.31, bf16[16,8,4096]{2,1,0:T(8,128)(2,1)} %bitcast.32, f32[1,4096]{1,0:T(1,128)} %bitcast.24, f32[1,4096]{1,0:T(1,128)} %bitcast.26), custom_call_target="tpu_custom_call" | custom-call | tf_op jit(solution)/shard_map/pack/pallas_call | solution.py:91
  4.4 0.0 copy-start.5
  4.4 115.2 %all_to_all.10 = bf16[256,4,8,256]{3,2,1,0:T(8,128)(2,1)S(1)} all-to-all(bf16[256,4,8,256]{3,2,1,0:T(8,128)(2,1)S(1)} %bitcast.19), channel_id=1, replica_groups=mesh['grp'=16,'sp'=16] {'grp','sp'}, dimensions={0} | all-to-all | bytes 8388608 | tf_op jit(solution)/shard_map/all_to_all | solution.py:245
  119.6 0.0 copy-done.5
  119.6 21.9 %attention.1 = bf16[16,16,4,8,256]{4,3,2,1,0:T(8,128)(2,1)S(1)} custom-call(s32[4]{0:T(128)S(1)} %bitcast.30, bf16[16,16,4,8,256]{4,3,2,1,0:T(8,128)(2,1)S(1)} %bitcast.17), custom_call_target="tpu_custom_call" | custom-call | tf_op jit(solution)/shard_map/attention/pallas_call | solution.py:177
  141.5 0.0 copy-start
  141.5 0.0 copy-start.1
  141.5 0.0 copy-start.2
  141.5 0.0 copy-start.3
  141.5 0.0 copy-start.4
  141.5 104.1 %all_to_all.11 = bf16[256,4,8,256]{3,2,1,0:T(8,128)(2,1)S(1)} all-to-all(bf16[256,4,8,256]{3,2,1,0:T(8,128)(2,1)S(1)} %bitcast.18), channel_id=1, replica_groups=mesh['grp'=16,'sp'=16] {'grp','sp'}, dimensions={0} | all-to-all | bytes 8388608 | tf_op jit(solution)/shard_map/all_to_all | solution.py:245
  245.6 0.0 copy-done
  245.6 0.0 copy-done.1
  245.6 0.0 copy-done.2
  245.6 0.0 copy-done.3
  245.6 0.0 copy-done.4
  245.6 3.9 %finish.1 = (bf16[16,8,4096]{2,1,0:T(8,128)(2,1)}, bf16[16,8,4096]{2,1,0:T(8,128)(2,1)}, bf16[16,8,4096]{2,1,0:T(8,128)(2,1)}, bf16[16,8,4096]{2,1,0:T(8,128)(2,1)}) custom-call(s32[16]{0:T(128)S(1)} %bitcast.29, bf16[16,16,4,8,256]{4,3,2,1,0:T(8,128)(2,1)S(1)} %bitcast.16, bf16[16,8,4096]{2,1,0:T(8,128)(2,1)S(1)} %bitcast.21, ...), custom_call_target="tpu_custom_call" | custom-call | tf_op jit(solution)/shard_map/finish/pallas_call | solution.py:229
Async XLA Ops:
  4.4 115.2 %copy-start.5 = (s32[1,4]{1,0:T(1,128)S(1)}, s32[1,4]{1,0:T(1,128)}, u32[]{:S(2)}) copy-start(s32[1,4]{1,0:T(1,128)} %param.14) | copy-start | bytes 52
  141.5 104.2 %copy-start = (bf16[128,4096]{1,0:T(8,128)(2,1)S(1)}, bf16[128,4096]{1,0:T(8,128)(2,1)}, u32[]{:S(2)}) copy-start(bf16[128,4096]{1,0:T(8,128)(2,1)} %param.8) | copy-start | bytes 3145732
  141.5 104.2 %copy-start.1 = (bf16[128,4096]{1,0:T(8,128)(2,1)S(1)}, bf16[128,4096]{1,0:T(8,128)(2,1)}, u32[]{:S(2)}) copy-start(bf16[128,4096]{1,0:T(8,128)(2,1)} %param.9) | copy-start | bytes 3145732
  141.5 104.1 %copy-start.2 = (f32[4096]{0:T(1024)S(1)}, f32[4096]{0:T(1024)}, u32[]{:S(2)}) copy-start(f32[4096]{0:T(1024)} %param.12) | copy-start | bytes 49156
  141.5 104.1 %copy-start.3 = (f32[4096]{0:T(1024)S(1)}, f32[4096]{0:T(1024)}, u32[]{:S(2)}) copy-start(f32[4096]{0:T(1024)} %param.13) | copy-start | bytes 49156
  141.5 104.1 %copy-start.4 = (s32[1,1,16]{2,1,0:T(1,128)S(1)}, s32[1,1,16]{2,1,0:T(1,128)}, u32[]{:S(2)}) copy-start(s32[1,1,16]{2,1,0:T(1,128)} %param.15) | copy-start | bytes 196

commit v4 on v3

--- a/solution.py
+++ b/solution.py
@@ -120,9 +120,9 @@
     dweights = lax.dot_general(c, values, rows, preferred_element_type=F32)
     dscores = (probs * (dweights - row_dot)).astype(BF16)
     d_query = jnp.dot(dscores, keys, preferred_element_type=F32) * SCALING
-    d_key = lax.dot_general(dscores, q, over_rows, preferred_element_type=F32) * SCALING
-    d_value = lax.dot_general(weights, c, over_rows, preferred_element_type=F32)
-    return attended, d_query, d_key, d_value
+    d_key = lax.dot_general(q, dscores, over_rows, preferred_element_type=F32) * SCALING
+    d_value = lax.dot_general(c, weights, over_rows, preferred_element_type=F32)
+    return attended, d_query, d_key.T, d_value.T
 
 
 def attention_kernel(frames, x_ref, out_ref, *held):
@@ -155,21 +155,25 @@
     def slab_rows(frame):
         return slice((frame % 2) * PER_FRAME, (frame % 2 + 1) * PER_FRAME)
 
+    for frame in range(FRAMES_GRP):
+        for which in range(4):
+            block = x_ref[slab_rows(frame), frame // 2, which].astype(F32)
+            block = block.reshape(TOK_FRAME, PAIR).astype(BF16)
+            for head in range(2):
+                lanes = slice(head * HDIM, (head + 1) * HDIM)
+                held[8 * head + which][slots[frame], :] = block[:, lanes]
     for head in range(2):
-        lanes = slice(head * HDIM, (head + 1) * HDIM)
         ins, outs = held[8 * head : 8 * head + 4], held[8 * head + 4 : 8 * head + 8]
-        for frame in range(FRAMES_GRP):
-            for which in range(4):
-                block = x_ref[slab_rows(frame), frame // 2, which, :, lanes].astype(F32)
-                ins[which][slots[frame], :] = block.reshape(TOK_FRAME, HDIM).astype(BF16)
         for section, mask in ((slice(0, BIG), None), (slice(BIG, S_GRP), same)):
             results = attend(*(ref[section, :] for ref in ins), mask)
             for which in range(4):
-                outs[which][section, :] = results[which].astype(outs[which].dtype)
-        for frame in range(FRAMES_GRP):
-            for which in range(4):
-                block = outs[which][slots[frame], :].astype(F32).reshape(PER_FRAME, SLAB, HDIM)
-                out_ref[slab_rows(frame), frame // 2, which, :, lanes] = block.astype(BF16)
+                outs[which][section, :] = results[which].astype(BF16)
+    for frame in range(FRAMES_GRP):
+        for which in range(4):
+            pair = [held[8 * head + 4 + which][slots[frame], :] for head in range(2)]
+            block = jnp.concatenate(pair, axis=1).astype(F32)
+            block = block.reshape(PER_FRAME, SLAB, PAIR)
+            out_ref[slab_rows(frame), frame // 2, which] = block.astype(BF16)
 
 
 def attention(frames, received):

time: 250 us -> 248 us (level)
  no operation moved by 1% of the time
where the time goes in v4:
time: 248 us
  blocking collectives  219 us (88%)
  Pallas kernels  27.4 us (11%)
    all_to_all x2, blocking collectives, exchange(): lax.all_to_all(flat, ('grp', 'sp'), split_axis=0, concat_axis=0, tiled=True)  219 us
    pallas_call x1, Pallas kernels, attention(): pl.pallas_call(attention_kernel, in_specs=[pl.BlockSpec(memory_space=pltp...  19.7 us

profile of v4, /device:TPU:1, one launch (start us, length us, event | category | flops | bytes accessed | tf_op | source)
XLA Modules:
  0.0 247.6 jit_solution(10034301905126310673)
XLA Ops:
  0.6 3.7 %pack.1 = bf16[16,16,4,8,256]{4,3,2,1,0:T(8,128)(2,1)S(1)} custom-call(s32[16]{0:T(128)} %bitcast.28, bf16[16,8,4096]{2,1,0:T(8,128)(2,1)} %bitcast.20, bf16[16,8,4096]{2,1,0:T(8,128)(2,1)} %bitcast.22, bf16[16,8,4096]{2,1,0:T(8,128)(2,1)} %bitcast.31, bf16[16,8,4096]{2,1,0:T(8,128)(2,1)} %bitcast.32, f32[1,4096]{1,0:T(1,128)} %bitcast.24, f32[1,4096]{1,0:T(1,128)} %bitcast.26), custom_call_target="tpu_custom_call" | custom-call | tf_op jit(solution)/shard_map/pack/pallas_call | solution.py:91
  4.3 0.0 copy-start.5
  4.4 115.2 %all_to_all.10 = bf16[256,4,8,256]{3,2,1,0:T(8,128)(2,1)S(1)} all-to-all(bf16[256,4,8,256]{3,2,1,0:T(8,128)(2,1)S(1)} %bitcast.19), channel_id=1, replica_groups=mesh['grp'=16,'sp'=16] {'grp','sp'}, dimensions={0} | all-to-all | bytes 8388608 | tf_op jit(solution)/shard_map/all_to_all | solution.py:249
  119.5 0.0 copy-done.5
  119.5 19.7 %attention.1 = bf16[16,16,4,8,256]{4,3,2,1,0:T(8,128)(2,1)S(1)} custom-call(s32[4]{0:T(128)S(1)} %bitcast.30, bf16[16,16,4,8,256]{4,3,2,1,0:T(8,128)(2,1)S(1)} %bitcast.17), custom_call_target="tpu_custom_call" | custom-call | tf_op jit(solution)/shard_map/attention/pallas_call | solution.py:181
  139.3 0.0 copy-start
  139.3 0.0 copy-start.1
  139.3 0.0 copy-start.2
  139.3 0.0 copy-start.3
  139.3 0.0 copy-start.4
  139.3 104.1 %all_to_all.11 = bf16[256,4,8,256]{3,2,1,0:T(8,128)(2,1)S(1)} all-to-all(bf16[256,4,8,256]{3,2,1,0:T(8,128)(2,1)S(1)} %bitcast.18), channel_id=1, replica_groups=mesh['grp'=16,'sp'=16] {'grp','sp'}, dimensions={0} | all-to-all | bytes 8388608 | tf_op jit(solution)/shard_map/all_to_all | solution.py:249
  243.4 0.0 copy-done
  243.4 0.0 copy-done.1
  243.4 0.0 copy-done.2
  243.4 0.0 copy-done.3
  243.5 0.0 copy-done.4
  243.5 3.9 %finish.1 = (bf16[16,8,4096]{2,1,0:T(8,128)(2,1)}, bf16[16,8,4096]{2,1,0:T(8,128)(2,1)}, bf16[16,8,4096]{2,1,0:T(8,128)(2,1)}, bf16[16,8,4096]{2,1,0:T(8,128)(2,1)}) custom-call(s32[16]{0:T(128)S(1)} %bitcast.29, bf16[16,16,4,8,256]{4,3,2,1,0:T(8,128)(2,1)S(1)} %bitcast.16, bf16[16,8,4096]{2,1,0:T(8,128)(2,1)S(1)} %bitcast.21, ...), custom_call_target="tpu_custom_call" | custom-call | tf_op jit(solution)/shard_map/finish/pallas_call | solution.py:233
Async XLA Ops:
  4.3 115.2 %copy-start.5 = (s32[1,4]{1,0:T(1,128)S(1)}, s32[1,4]{1,0:T(1,128)}, u32[]{:S(2)}) copy-start(s32[1,4]{1,0:T(1,128)} %param.14) | copy-start | bytes 52
  139.3 104.2 %copy-start = (bf16[128,4096]{1,0:T(8,128)(2,1)S(1)}, bf16[128,4096]{1,0:T(8,128)(2,1)}, u32[]{:S(2)}) copy-start(bf16[128,4096]{1,0:T(8,128)(2,1)} %param.8) | copy-start | bytes 3145732
  139.3 104.2 %copy-start.1 = (bf16[128,4096]{1,0:T(8,128)(2,1)S(1)}, bf16[128,4096]{1,0:T(8,128)(2,1)}, u32[]{:S(2)}) copy-start(bf16[128,4096]{1,0:T(8,128)(2,1)} %param.9) | copy-start | bytes 3145732
  139.3 104.1 %copy-start.2 = (f32[4096]{0:T(1024)S(1)}, f32[4096]{0:T(1024)}, u32[]{:S(2)}) copy-start(f32[4096]{0:T(1024)} %param.12) | copy-start | bytes 49156
  139.3 104.1 %copy-start.3 = (f32[4096]{0:T(1024)S(1)}, f32[4096]{0:T(1024)}, u32[]{:S(2)}) copy-start(f32[4096]{0:T(1024)} %param.13) | copy-start | bytes 49156
  139.3 104.1 %copy-start.4 = (s32[1,1,16]{2,1,0:T(1,128)S(1)}, s32[1,1,16]{2,1,0:T(1,128)}, u32[]{:S(2)}) copy-start(s32[1,1,16]{2,1,0:T(1,128)} %param.15) | copy-start | bytes 196

commit v5 on v4

--- a/solution.py
+++ b/solution.py
@@ -21,7 +21,7 @@
 REST = S_GRP - BIG
 PER_FRAME = TOK_FRAME // SLAB
 PAIR = 2 * HDIM
-PART = 4
+PART = 8
 
 EPSILON = 1e-06
 MASKED = -1e30
@@ -39,7 +39,20 @@
 
 
 def pack_kernel(
-    dest, q_ref, k_ref, v_ref, c_ref, qg_hbm, kg_hbm, out_ref, held, qg_ref, kg_ref, arrived, ready
+    dest,
+    q_ref,
+    k_ref,
+    v_ref,
+    c_ref,
+    qg_hbm,
+    kg_hbm,
+    out_ref,
+    factor_ref,
+    held,
+    qg_ref,
+    kg_ref,
+    arrived,
+    ready,
 ):
     gains = (
         pltpu.make_async_copy(qg_hbm, qg_ref, ready.at[0]),
@@ -60,17 +73,19 @@
     for copy in gains:
         copy.wait()
 
-    def normalize(values, gain_ref):
-        wide = values.astype(F32)
-        return (wide * rms_factor(wide) * gain_ref[...]).astype(BF16)
+    def normalize(which, slab, gain_ref):
+        wide = held[which, slab].astype(F32)
+        factor = rms_factor(wide)
+        factor_ref[which, slab] = jnp.broadcast_to(factor, (SLAB, HDIM))
+        return (wide * factor * gain_ref[...]).astype(BF16)
 
     for part in range(N_GRP // PART):
         for which in range(4):
             fetch(which, part).wait()
         for slab in range(part * PART, (part + 1) * PART):
             rows = (
-                normalize(held[0, slab], qg_ref),
-                normalize(held[1, slab], kg_ref),
+                normalize(0, slab, qg_ref),
+                normalize(1, slab, kg_ref),
                 held[2, slab],
                 held[3, slab],
             )
@@ -91,8 +106,11 @@
     return pl.pallas_call(
         pack_kernel,
         in_specs=[smem, hbm, hbm, hbm, hbm, hbm, hbm],
-        out_specs=vmem,
-        out_shape=jax.ShapeDtypeStruct((N_GRP, N_SP, 4, SLAB, PAIR), BF16),
+        out_specs=[vmem, vmem],
+        out_shape=[
+            jax.ShapeDtypeStruct((N_GRP, N_SP, 4, SLAB, PAIR), BF16),
+            jax.ShapeDtypeStruct((2, N_GRP, SLAB, HDIM), F32),
+        ],
         scratch_shapes=[
             pltpu.VMEM((4, N_GRP, SLAB, WIDTH), BF16),
             pltpu.VMEM((1, WIDTH), F32),
@@ -167,17 +185,18 @@
         for section, mask in ((slice(0, BIG), None), (slice(BIG, S_GRP), same)):
             results = attend(*(ref[section, :] for ref in ins), mask)
             for which in range(4):
-                outs[which][section, :] = results[which].astype(BF16)
+                outs[which][section, :] = results[which].astype(F32)
     for frame in range(FRAMES_GRP):
         for which in range(4):
             pair = [held[8 * head + 4 + which][slots[frame], :] for head in range(2)]
-            block = jnp.concatenate(pair, axis=1).astype(F32)
+            block = jnp.concatenate(pair, axis=1)
             block = block.reshape(PER_FRAME, SLAB, PAIR)
             out_ref[slab_rows(frame), frame // 2, which] = block.astype(BF16)
 
 
 def attention(frames, received):
-    held = [pltpu.VMEM((S_GRP, HDIM), BF16)] * 16
+    kept = [pltpu.VMEM((S_GRP, HDIM), BF16)] * 4 + [pltpu.VMEM((S_GRP, HDIM), F32)] * 4
+    held = kept + kept
     return pl.pallas_call(
         attention_kernel,
         in_specs=[
@@ -193,16 +212,27 @@
 
 
 def finish_kernel(
-    dest, x_ref, q_ref, k_ref, qg_ref, kg_ref, att_ref, gq_ref, gk_ref, gv_ref, held, gone
+    dest,
+    x_ref,
+    factor_ref,
+    q_ref,
+    k_ref,
+    qg_ref,
+    kg_ref,
+    att_ref,
+    gq_ref,
+    gk_ref,
+    gv_ref,
+    held,
+    gone,
 ):
     def store(which, part):
         target = (att_ref, gq_ref, gk_ref, gv_ref)[which]
         rows = pl.ds(part * PART, PART)
         return pltpu.make_async_copy(held.at[which, rows], target.at[rows], gone.at[which, part])
 
-    def normalize_back(values, gain_ref, upstream):
+    def normalize_back(values, factor, gain_ref, upstream):
         wide = values.astype(F32)
-        factor = rms_factor(wide)
         scaled = gain_ref[...] * upstream.astype(F32)
         inner = jnp.mean(wide * scaled, axis=-1, keepdims=True)
         return (factor * scaled - wide * (factor * factor * factor * inner)).astype(BF16)
@@ -219,20 +249,22 @@
             for slab in range(part * PART, (part + 1) * PART):
                 pieces = [x_ref[dest[slab], owner, which] for owner in range(N_SP)]
                 upstream = jnp.concatenate(pieces, axis=1)
-                held[which, slab] = normalize_back(source[slab], gain_ref, upstream)
+                held[which, slab] = normalize_back(
+                    source[slab], factor_ref[which - 1, slab][:, :1], gain_ref, upstream
+                )
             store(which, part).start()
     for part in range(N_GRP // PART):
         for which in range(4):
             store(which, part).wait()
 
 
-def finish(dest, returned, query_in, key_in, query_gain, key_gain):
+def finish(dest, returned, factors, query_in, key_in, query_gain, key_gain):
     smem = pl.BlockSpec(memory_space=pltpu.SMEM)
     vmem = pl.BlockSpec(memory_space=pltpu.VMEM)
     hbm = pl.BlockSpec(memory_space=pl.ANY)
     return pl.pallas_call(
         finish_kernel,
-        in_specs=[smem, vmem, vmem, vmem, vmem, vmem],
+        in_specs=[smem, vmem, vmem, vmem, vmem, vmem, vmem],
         out_specs=[hbm, hbm, hbm, hbm],
         out_shape=[jax.ShapeDtypeStruct((N_GRP, SLAB, WIDTH), BF16)] * 4,
         scratch_shapes=[
@@ -241,7 +273,7 @@
         ],
         compiler_params=pltpu.CompilerParams(vmem_limit_bytes=32 * MIB),
         name="finish",
-    )(dest, returned, query_in, key_in, query_gain, key_gain)
+    )(dest, returned, factors, query_in, key_in, query_gain, key_gain)
 
 
 def exchange(values):
@@ -258,11 +290,11 @@
         return values.reshape(N_GRP, SLAB, width)
 
     gains = (query_gain.reshape(1, width), key_gain.reshape(1, width))
-    sent = pack(
+    sent, factors = pack(
         dest, slabs(query_in), slabs(key_in), slabs(value_in), slabs(out_cotangent), *gains
     )
     results = attention(frames.reshape(NVID), exchange(sent))
-    outputs = finish(dest, exchange(results), slabs(query_in), slabs(key_in), *gains)
+    outputs = finish(dest, exchange(results), factors, slabs(query_in), slabs(key_in), *gains)
     return tuple(values.reshape(tokens, width) for values in outputs)
 
 

time: 248 us -> 247 us (level)
  no operation moved by 1% of the time
where the time goes in v5:
time: 247 us
  blocking collectives  219 us (89%)
  Pallas kernels  26.7 us (11%)
    all_to_all x2, blocking collectives, exchange(): lax.all_to_all(flat, ('grp', 'sp'), split_axis=0, concat_axis=0, tiled=True)  219 us
    pallas_call x1, Pallas kernels, attention(): pl.pallas_call(attention_kernel, in_specs=[pl.BlockSpec(memory_space=pltp...  19.6 us

profile of v5, /device:TPU:1, one launch (start us, length us, event | category | flops | bytes accessed | tf_op | source)
XLA Modules:
  0.0 246.9 jit_solution(17807276461337935108)
XLA Ops:
  0.6 3.5 %pack.1 = (bf16[16,16,4,8,256]{4,3,2,1,0:T(8,128)(2,1)S(1)}, f32[2,16,8,128]{3,2,1,0:T(8,128)S(1)}) custom-call(s32[16]{0:T(128)} %bitcast.28, bf16[16,8,4096]{2,1,0:T(8,128)(2,1)} %bitcast.19, bf16[16,8,4096]{2,1,0:T(8,128)(2,1)} %bitcast.21, bf16[16,8,4096]{2,1,0:T(8,128)(2,1)} %bitcast.31, bf16[16,8,4096]{2,1,0:T(8,128)(2,1)} %bitcast.32, ...), custom_call_target="tpu_custom_call" | custom-call | tf_op jit(solution)/shard_map/pack/pallas_call | solution.py:106
  4.2 0.0 copy-start.5
  4.2 115.2 %all_to_all.10 = bf16[256,4,8,256]{3,2,1,0:T(8,128)(2,1)S(1)} all-to-all(bf16[256,4,8,256]{3,2,1,0:T(8,128)(2,1)S(1)} %bitcast.23), channel_id=1, replica_groups=mesh['grp'=16,'sp'=16] {'grp','sp'}, dimensions={0} | all-to-all | bytes 8388608 | tf_op jit(solution)/shard_map/all_to_all | solution.py:281
  119.3 0.0 copy-done.5
  119.3 19.6 %attention.1 = bf16[16,16,4,8,256]{4,3,2,1,0:T(8,128)(2,1)S(1)} custom-call(s32[4]{0:T(128)S(1)} %bitcast.30, bf16[16,16,4,8,256]{4,3,2,1,0:T(8,128)(2,1)S(1)} %bitcast.17), custom_call_target="tpu_custom_call" | custom-call | tf_op jit(solution)/shard_map/attention/pallas_call | solution.py:200
  139.0 0.0 copy-start
  139.0 0.0 copy-start.1
  139.0 0.0 copy-start.2
  139.0 0.0 copy-start.3
  139.0 0.0 copy-start.4
  139.0 104.1 %all_to_all.11 = bf16[256,4,8,256]{3,2,1,0:T(8,128)(2,1)S(1)} all-to-all(bf16[256,4,8,256]{3,2,1,0:T(8,128)(2,1)S(1)} %bitcast.18), channel_id=1, replica_groups=mesh['grp'=16,'sp'=16] {'grp','sp'}, dimensions={0} | all-to-all | bytes 8388608 | tf_op jit(solution)/shard_map/all_to_all | solution.py:281
  243.1 0.0 copy-done
  243.1 0.0 copy-done.1
  243.1 0.0 copy-done.2
  243.1 0.0 copy-done.3
  243.1 0.0 copy-done.4
  243.2 3.6 %finish.1 = (bf16[16,8,4096]{2,1,0:T(8,128)(2,1)}, bf16[16,8,4096]{2,1,0:T(8,128)(2,1)}, bf16[16,8,4096]{2,1,0:T(8,128)(2,1)}, bf16[16,8,4096]{2,1,0:T(8,128)(2,1)}) custom-call(s32[16]{0:T(128)S(1)} %bitcast.29, bf16[16,16,4,8,256]{4,3,2,1,0:T(8,128)(2,1)S(1)} %bitcast.16, f32[2,16,8,128]{3,2,1,0:T(8,128)S(1)} %get-tuple-element.11.factor_ref, ...), custom_call_target="tpu_custom_call" | custom-call | tf_op jit(solution)/shard_map/finish/pallas_call | solution.py:265
Async XLA Ops:
  4.2 115.2 %copy-start.5 = (s32[1,4]{1,0:T(1,128)S(1)}, s32[1,4]{1,0:T(1,128)}, u32[]{:S(2)}) copy-start(s32[1,4]{1,0:T(1,128)} %param.14) | copy-start | bytes 52
  139.0 104.2 %copy-start = (bf16[128,4096]{1,0:T(8,128)(2,1)S(1)}, bf16[128,4096]{1,0:T(8,128)(2,1)}, u32[]{:S(2)}) copy-start(bf16[128,4096]{1,0:T(8,128)(2,1)} %param.8) | copy-start | bytes 3145732
  139.0 104.2 %copy-start.1 = (bf16[128,4096]{1,0:T(8,128)(2,1)S(1)}, bf16[128,4096]{1,0:T(8,128)(2,1)}, u32[]{:S(2)}) copy-start(bf16[128,4096]{1,0:T(8,128)(2,1)} %param.9) | copy-start | bytes 3145732
  139.0 104.1 %copy-start.2 = (f32[4096]{0:T(1024)S(1)}, f32[4096]{0:T(1024)}, u32[]{:S(2)}) copy-start(f32[4096]{0:T(1024)} %param.12) | copy-start | bytes 49156
  139.0 104.1 %copy-start.3 = (f32[4096]{0:T(1024)S(1)}, f32[4096]{0:T(1024)}, u32[]{:S(2)}) copy-start(f32[4096]{0:T(1024)} %param.13) | copy-start | bytes 49156
  139.0 104.1 %copy-start.4 = (s32[1,1,16]{2,1,0:T(1,128)S(1)}, s32[1,1,16]{2,1,0:T(1,128)}, u32[]{:S(2)}) copy-start(s32[1,1,16]{2,1,0:T(1,128)} %param.15) | copy-start | bytes 196

commit v6 on v5

--- a/solution.py
+++ b/solution.py
@@ -22,6 +22,7 @@
 PER_FRAME = TOK_FRAME // SLAB
 PAIR = 2 * HDIM
 PART = 8
+HOME_PART = 4
 
 EPSILON = 1e-06
 MASKED = -1e30
@@ -65,11 +66,11 @@
             source.at[rows], held.at[which, rows], arrived.at[which, part]
         )
 
-    for copy in gains:
-        copy.start()
     for part in range(N_GRP // PART):
         for which in range(4):
             fetch(which, part).start()
+            if part == 0 and which < 2:
+                gains[which].start()
     for copy in gains:
         copy.wait()
 
@@ -228,7 +229,7 @@
 ):
     def store(which, part):
         target = (att_ref, gq_ref, gk_ref, gv_ref)[which]
-        rows = pl.ds(part * PART, PART)
+        rows = pl.ds(part * HOME_PART, HOME_PART)
         return pltpu.make_async_copy(held.at[which, rows], target.at[rows], gone.at[which, part])
 
     def normalize_back(values, factor, gain_ref, upstream):
@@ -237,23 +238,23 @@
         inner = jnp.mean(wide * scaled, axis=-1, keepdims=True)
         return (factor * scaled - wide * (factor * factor * factor * inner)).astype(BF16)
 
-    for part in range(N_GRP // PART):
+    for part in range(N_GRP // HOME_PART):
         for which in (0, 3):
-            for slab in range(part * PART, (part + 1) * PART):
+            for slab in range(part * HOME_PART, (part + 1) * HOME_PART):
                 for owner in range(N_SP):
                     columns = slice(owner * PAIR, (owner + 1) * PAIR)
                     held[which, slab, :, columns] = x_ref[dest[slab], owner, which]
             store(which, part).start()
-    for part in range(N_GRP // PART):
+    for part in range(N_GRP // HOME_PART):
         for which, source, gain_ref in ((1, q_ref, qg_ref), (2, k_ref, kg_ref)):
-            for slab in range(part * PART, (part + 1) * PART):
+            for slab in range(part * HOME_PART, (part + 1) * HOME_PART):
                 pieces = [x_ref[dest[slab], owner, which] for owner in range(N_SP)]
                 upstream = jnp.concatenate(pieces, axis=1)
                 held[which, slab] = normalize_back(
                     source[slab], factor_ref[which - 1, slab][:, :1], gain_ref, upstream
                 )
             store(which, part).start()
-    for part in range(N_GRP // PART):
+    for part in range(N_GRP // HOME_PART):
         for which in range(4):
             store(which, part).wait()
 
@@ -269,7 +270,7 @@
         out_shape=[jax.ShapeDtypeStruct((N_GRP, SLAB, WIDTH), BF16)] * 4,
         scratch_shapes=[
             pltpu.VMEM((4, N_GRP, SLAB, WIDTH), BF16),
-            pltpu.SemaphoreType.DMA((4, N_GRP // PART)),
+            pltpu.SemaphoreType.DMA((4, N_GRP // HOME_PART)),
         ],
         compiler_params=pltpu.CompilerParams(vmem_limit_bytes=32 * MIB),
         name="finish",

time: 247 us -> 247 us (level)
  no operation moved by 1% of the time
where the time goes in v6:
time: 247 us
  blocking collectives  219 us (89%)
  Pallas kernels  26.7 us (11%)
    all_to_all x2, blocking collectives, exchange(): lax.all_to_all(flat, ('grp', 'sp'), split_axis=0, concat_axis=0, tiled=True)  219 us
    pallas_call x1, Pallas kernels, attention(): pl.pallas_call(attention_kernel, in_specs=[pl.BlockSpec(memory_space=pltp...  19.6 us

profile of v6, /device:TPU:1, one launch (start us, length us, event | category | flops | bytes accessed | tf_op | source)
XLA Modules:
  0.0 246.9 jit_solution(18051511162250347701)
XLA Ops:
  0.6 3.5 %pack.1 = (bf16[16,16,4,8,256]{4,3,2,1,0:T(8,128)(2,1)S(1)}, f32[2,16,8,128]{3,2,1,0:T(8,128)S(1)}) custom-call(s32[16]{0:T(128)} %bitcast.28, bf16[16,8,4096]{2,1,0:T(8,128)(2,1)} %bitcast.19, bf16[16,8,4096]{2,1,0:T(8,128)(2,1)} %bitcast.21, bf16[16,8,4096]{2,1,0:T(8,128)(2,1)} %bitcast.31, bf16[16,8,4096]{2,1,0:T(8,128)(2,1)} %bitcast.32, ...), custom_call_target="tpu_custom_call" | custom-call | tf_op jit(solution)/shard_map/pack/pallas_call | solution.py:107
  4.2 0.0 copy-start.5
  4.2 115.2 %all_to_all.10 = bf16[256,4,8,256]{3,2,1,0:T(8,128)(2,1)S(1)} all-to-all(bf16[256,4,8,256]{3,2,1,0:T(8,128)(2,1)S(1)} %bitcast.23), channel_id=1, replica_groups=mesh['grp'=16,'sp'=16] {'grp','sp'}, dimensions={0} | all-to-all | bytes 8388608 | tf_op jit(solution)/shard_map/all_to_all | solution.py:282
  119.3 0.0 copy-done.5
  119.3 19.6 %attention.1 = bf16[16,16,4,8,256]{4,3,2,1,0:T(8,128)(2,1)S(1)} custom-call(s32[4]{0:T(128)S(1)} %bitcast.30, bf16[16,16,4,8,256]{4,3,2,1,0:T(8,128)(2,1)S(1)} %bitcast.17), custom_call_target="tpu_custom_call" | custom-call | tf_op jit(solution)/shard_map/attention/pallas_call | solution.py:201
  139.0 0.0 copy-start
  139.0 0.0 copy-start.1
  139.0 0.0 copy-start.2
  139.0 0.0 copy-start.3
  139.0 0.0 copy-start.4
  139.0 104.1 %all_to_all.11 = bf16[256,4,8,256]{3,2,1,0:T(8,128)(2,1)S(1)} all-to-all(bf16[256,4,8,256]{3,2,1,0:T(8,128)(2,1)S(1)} %bitcast.18), channel_id=1, replica_groups=mesh['grp'=16,'sp'=16] {'grp','sp'}, dimensions={0} | all-to-all | bytes 8388608 | tf_op jit(solution)/shard_map/all_to_all | solution.py:282
  243.1 0.0 copy-done
  243.1 0.0 copy-done.1
  243.1 0.0 copy-done.2
  243.1 0.0 copy-done.3
  243.1 0.0 copy-done.4
  243.2 3.6 %finish.1 = (bf16[16,8,4096]{2,1,0:T(8,128)(2,1)}, bf16[16,8,4096]{2,1,0:T(8,128)(2,1)}, bf16[16,8,4096]{2,1,0:T(8,128)(2,1)}, bf16[16,8,4096]{2,1,0:T(8,128)(2,1)}) custom-call(s32[16]{0:T(128)S(1)} %bitcast.29, bf16[16,16,4,8,256]{4,3,2,1,0:T(8,128)(2,1)S(1)} %bitcast.16, f32[2,16,8,128]{3,2,1,0:T(8,128)S(1)} %get-tuple-element.11.factor_ref, ...), custom_call_target="tpu_custom_call" | custom-call | tf_op jit(solution)/shard_map/finish/pallas_call | solution.py:266
Async XLA Ops:
  4.2 115.2 %copy-start.5 = (s32[1,4]{1,0:T(1,128)S(1)}, s32[1,4]{1,0:T(1,128)}, u32[]{:S(2)}) copy-start(s32[1,4]{1,0:T(1,128)} %param.14) | copy-start | bytes 52
  139.0 104.2 %copy-start = (bf16[128,4096]{1,0:T(8,128)(2,1)S(1)}, bf16[128,4096]{1,0:T(8,128)(2,1)}, u32[]{:S(2)}) copy-start(bf16[128,4096]{1,0:T(8,128)(2,1)} %param.8) | copy-start | bytes 3145732
  139.0 104.2 %copy-start.1 = (bf16[128,4096]{1,0:T(8,128)(2,1)S(1)}, bf16[128,4096]{1,0:T(8,128)(2,1)}, u32[]{:S(2)}) copy-start(bf16[128,4096]{1,0:T(8,128)(2,1)} %param.9) | copy-start | bytes 3145732
  139.0 104.1 %copy-start.2 = (f32[4096]{0:T(1024)S(1)}, f32[4096]{0:T(1024)}, u32[]{:S(2)}) copy-start(f32[4096]{0:T(1024)} %param.12) | copy-start | bytes 49156
  139.0 104.1 %copy-start.3 = (f32[4096]{0:T(1024)S(1)}, f32[4096]{0:T(1024)}, u32[]{:S(2)}) copy-start(f32[4096]{0:T(1024)} %param.13) | copy-start | bytes 49156
  139.0 104.1 %copy-start.4 = (s32[1,1,16]{2,1,0:T(1,128)S(1)}, s32[1,1,16]{2,1,0:T(1,128)}, u32[]{:S(2)}) copy-start(s32[1,1,16]{2,1,0:T(1,128)} %param.15) | copy-start | bytes 196
